TPU v7x, 32 devices: a whole 2x2x4 slice. The times are simulated.
32 devices in a mesh: batch: 4 (over y, x), seq: 8 (over z, core).
Axes of the slice: x: 2, y: 2, z: 4, core: 2. Of those that a mesh axis runs over, the one named last changes fastest.
Arguments:
- tokens: bfloat16 [8, 2048, 768], P('batch', 'seq'), may hold values from -6 to 6
- neighbours: bfloat16 [8, 32, 2, 128, 768], P('batch', 'seq'), may hold values from -6 to 6
- present: int32 [8, 32, 2], P('batch', 'seq'), may hold values 0 or 1
- qkv_weight: bfloat16 [768, 2304], replicated, may hold values from -0.21875 to 0.21875
- attn_weight: bfloat16 [768, 768], replicated, may hold values from -1.75 to 1.75
- query_weight: bfloat16 [768, 768], replicated, may hold values from -0.21875 to 0.21875
- memory_weight: bfloat16 [768, 1536], replicated, may hold values from -0.21875 to 0.21875
- cross_weight: bfloat16 [768, 768], replicated, may hold values from -1.75 to 1.75
- up_weight: bfloat16 [768, 3072], replicated, may hold values from -0.21875 to 0.21875
- down_weight: bfloat16 [3072, 768], replicated, may hold values from -0.109375 to 0.109375
- attn_gain: float32 [768], replicated, may hold values from 0.1 to 1.9
- attn_shift: float32 [768], replicated, may hold values from -1.2 to 1.2
- cross_gain: float32 [768], replicated, may hold values from 0.1 to 1.9
- cross_shift: float32 [768], replicated, may hold values from -1.2 to 1.2
- mlp_gain: float32 [768], replicated, may hold values from 0.1 to 1.9
- mlp_shift: float32 [768], replicated, may hold values from -1.2 to 1.2
- cotangent: bfloat16 [8, 2048, 768], P('batch', 'seq'), may hold values from -6 to 6
Outputs:
- output: bfloat16 [8, 2048, 768], P('batch', 'seq')
- grad_tokens: bfloat16 [8, 2048, 768], P('batch', 'seq')
- grad_neighbours: bfloat16 [8, 32, 2, 128, 768], P('batch', 'seq')
- grad_qkv: float32 [768, 2304], P('seq')
- grad_attn: float32 [768, 768], P('seq')
- grad_query: float32 [768, 768], P('seq')
- grad_memory: float32 [768, 1536], P('seq')
- grad_cross: float32 [768, 768], P('seq')
- grad_up: float32 [768, 3072], P('seq')
- grad_down: float32 [3072, 768], P('seq')
- grad_attn_gain: float32 [768], P('seq')
- grad_attn_shift: float32 [768], P('seq')
- grad_cross_gain: float32 [768], P('seq')
- grad_cross_shift: float32 [768], P('seq')
- grad_mlp_gain: float32 [768], P('seq')
- grad_mlp_shift: float32 [768], P('seq')
Inputs may be any that keep to these rules, and one draw needn't show every extreme that they name: `present`: 1 marks a retrieved neighbour of the window, 0 one that is absent.
All inputs are finite; a program needn't handle non-finite values. No bound on the sum of `present` on one device may be relied on, other than what follows from the above.
Results may differ from a plain program's by a relative error of at most 0.028.
Values may be sent and summed in bfloat16 or wider, within the bound.
No kernel may reach another device: no remote copies, remote signals or barrier semaphores. Data moves between devices by JAX's collectives and lax.ppermute only.
A program may use at most 512 MiB of HBM per device.

v0:
```python
import math

import jax
import jax.numpy as jnp
from jax import lax
from jax.sharding import PartitionSpec as P

D = 768
HEADS = 12
HD = 64
GROUP = 64
NEIGH = 2
RET = 128


EPSILON = 1e-05
NEGATIVE = -1e30


def from_behind(value, axis, by):
    peers = lax.axis_size(axis)
    pairs = [(i, i + by) for i in range(peers) if 0 <= i + by < peers]
    return lax.ppermute(value, axis, pairs)


def norm_rows(values, gain_vec, shift_vec):
    row_mean = jnp.mean(values, axis=-1, keepdims=True)
    centred = values - row_mean
    variance = jnp.mean(centred * centred, axis=-1, keepdims=True)
    return centred * lax.rsqrt(variance + EPSILON) * gain_vec + shift_vec


def rotate(values, positions, direction):
    half_dim = HD // 2
    frequency = 10000.0 ** (-jnp.arange(half_dim, dtype=jnp.float32) * 2.0 / HD)
    angles = positions.astype(jnp.float32)[:, None] * frequency[None, :]
    cosine = jnp.cos(angles)[:, None, :]
    sine_part = direction * jnp.sin(angles)[:, None, :]
    first_half = values[..., :half_dim]
    second_half = values[..., half_dim:]
    return jnp.concatenate(
        [
            first_half * cosine - second_half * sine_part,
            second_half * cosine + first_half * sine_part,
        ],
        axis=-1,
    )


def gelu_exact(values):
    return jax.nn.gelu(values, approximate=False)


def matmul(left, right):
    return jnp.dot(left, right, preferred_element_type=jnp.float32)


def matmul_back(left, right):
    return lax.dot_general(
        left, right, (((1,), (1,)), ((), ())), preferred_element_type=jnp.float32
    )


def matmul_rows(left, right):
    return lax.dot_general(
        left, right, (((0,), (0,)), ((), ())), preferred_element_type=jnp.float32
    )


def collect_keys(keys_own, values_own):
    return (
        lax.all_gather(keys_own, "seq", axis=1, tiled=True),
        lax.all_gather(values_own, "seq", axis=1, tiled=True),
    )


def attend_piece(carried, queries, query_positions, query_last, key_rows, value_rows):
    seq_count = queries.shape[0]
    width_keys = key_rows.shape[1]
    block_len = math.gcd(width_keys, 512)
    score_scale = 1.0 / math.sqrt(HD)

    def attend_visit_block(step_index, running):
        key_start = step_index * block_len

        def attend_compute(state_now):
            row_max, row_total, weighted = state_now
            key_block = lax.dynamic_slice_in_dim(
                key_rows, step_index * block_len, block_len, 1
            ).reshape(seq_count, block_len, HEADS, HD)
            value_block = lax.dynamic_slice_in_dim(
                value_rows, step_index * block_len, block_len, 1
            ).reshape(seq_count, block_len, HEADS, HD)
            scores = (
                jnp.einsum(
                    "sthd,skhd->sthk", queries, key_block, preferred_element_type=jnp.float32
                )
                * score_scale
            )
            key_positions = key_start + jnp.arange(block_len, dtype=jnp.int32)
            allowed = (key_positions[None, :] <= query_positions[:, None])[None, :, None, :]
            masked = jnp.where(allowed, scores, NEGATIVE)
            new_max = jnp.maximum(row_max, jnp.max(masked, axis=-1))
            weights_exp = jnp.where(allowed, jnp.exp(masked - new_max[..., None]), 0.0)
            factor = jnp.exp(row_max - new_max)
            row_total = row_total * factor + jnp.sum(weights_exp, axis=-1)
            weighted = weighted * factor[..., None] + jnp.einsum(
                "sthk,skhd->sthd",
                weights_exp.astype(jnp.bfloat16),
                value_block,
                preferred_element_type=jnp.float32,
            )
            return (new_max, row_total, weighted)

        return lax.cond(
            key_start <= query_last, attend_compute, lambda state_now: state_now, running
        )

    return lax.fori_loop(0, width_keys // block_len, attend_visit_block, carried)


def block_grads(
    queries, grad_heads, delta, log_total, query_positions, key_start, key_block, value_block
):
    score_scale = 1.0 / math.sqrt(HD)
    scores = (
        jnp.einsum("sthd,skhd->sthk", queries, key_block, preferred_element_type=jnp.float32)
        * score_scale
    )
    key_positions = key_start + jnp.arange(key_block.shape[1], dtype=jnp.int32)
    allowed = (key_positions[None, :] <= query_positions[:, None])[None, :, None, :]
    probability = jnp.exp(jnp.where(allowed, scores - log_total[..., None], NEGATIVE))
    grad_prob = jnp.einsum(
        "sthd,skhd->sthk", grad_heads, value_block, preferred_element_type=jnp.float32
    )
    grad_score = (probability * (grad_prob - delta[..., None])).astype(jnp.bfloat16)
    return (probability, grad_score)


def query_grads(
    queries, grad_heads, delta, log_total, query_positions, query_last, keys_all, values_all
):
    seq_count = queries.shape[0]
    length = keys_all.shape[1]
    block_len = math.gcd(length, 512)

    def query_visit_block(step_index, running):
        key_start = step_index * block_len

        def query_compute(summed):
            key_block = lax.dynamic_slice_in_dim(keys_all, key_start, block_len, 1).reshape(
                seq_count, block_len, HEADS, HD
            )
            value_block = lax.dynamic_slice_in_dim(values_all, key_start, block_len, 1).reshape(
                seq_count, block_len, HEADS, HD
            )
            probability, grad_score = block_grads(
                queries,
                grad_heads,
                delta,
                log_total,
                query_positions,
                key_start,
                key_block,
                value_block,
            )
            return summed + jnp.einsum(
                "sthk,skhd->sthd", grad_score, key_block, preferred_element_type=jnp.float32
            )

        return lax.cond(key_start <= query_last, query_compute, lambda summed: summed, running)

    return lax.fori_loop(
        0, length // block_len, query_visit_block, jnp.zeros(queries.shape, jnp.float32)
    )


def shards(
    tokens,
    neighbours,
    present,
    qkv_weight,
    attn_weight,
    query_weight,
    memory_weight,
    cross_weight,
    up_weight,
    down_weight,
    attn_gain,
    attn_shift,
    cross_gain,
    cross_shift,
    mlp_gain,
    mlp_shift,
    cotangent,
):
    seq_count = tokens.shape[0]
    tok_rows = tokens.shape[1]
    all_rows = seq_count * tok_rows
    group_count = neighbours.shape[1]
    seq_index = lax.axis_index("seq")
    query_positions = seq_index * tok_rows + jnp.arange(tok_rows, dtype=jnp.int32)
    query_last = seq_index * tok_rows + (tok_rows - 1)
    score_scale = 1.0 / math.sqrt(HD)
    token_vals = tokens.astype(jnp.float32).reshape(all_rows, D)
    normed_one = norm_rows(token_vals, attn_gain, attn_shift).astype(jnp.bfloat16)
    projected = matmul(normed_one, qkv_weight).reshape(seq_count, tok_rows, 3, HEADS, HD)
    queries = rotate(projected[:, :, 0], query_positions, 1.0).astype(jnp.bfloat16)
    keys_own = (
        rotate(projected[:, :, 1], query_positions, 1.0)
        .astype(jnp.bfloat16)
        .reshape(seq_count, tok_rows, D)
    )
    values_own = projected[:, :, 2].astype(jnp.bfloat16).reshape(seq_count, tok_rows, D)
    start_state = (
        jnp.full((seq_count, tok_rows, HEADS), NEGATIVE, jnp.float32),
        jnp.zeros((seq_count, tok_rows, HEADS), jnp.float32),
        jnp.zeros((seq_count, tok_rows, HEADS, HD), jnp.float32),
    )
    row_max, row_total, weighted = attend_piece(
        start_state,
        queries,
        query_positions,
        query_last,
        lax.all_gather(keys_own, "seq", axis=1, tiled=True),
        lax.all_gather(values_own, "seq", axis=1, tiled=True),
    )
    attn_full = weighted / row_total[..., None]
    log_total = row_max + jnp.log(row_total)
    attn_low = attn_full.astype(jnp.bfloat16).reshape(all_rows, D)
    after_attn = token_vals + matmul(attn_low, attn_weight)
    normed_two = (
        norm_rows(after_attn, cross_gain, cross_shift)
        .astype(jnp.bfloat16)
        .reshape(seq_count, tok_rows, D)
    )
    before_rows = from_behind(normed_two[:, -1:, :], "seq", 1)
    shifted = jnp.concatenate([before_rows, normed_two[:, :-1, :]], axis=1).reshape(all_rows, D)
    cross_query = (
        matmul(shifted, query_weight)
        .astype(jnp.bfloat16)
        .reshape(seq_count, group_count, GROUP, HEADS, HD)
    )
    neigh_rows = neighbours.reshape(seq_count * group_count * NEIGH * RET, D)
    memory = (
        matmul(neigh_rows, memory_weight)
        .astype(jnp.bfloat16)
        .reshape(seq_count, group_count, NEIGH * RET, 2, HEADS, HD)
    )
    cross_keys = memory[:, :, :, 0]
    cross_values = memory[:, :, :, 1]
    allowed = jnp.repeat(present > 0, RET, axis=2)[:, :, None, None, :]
    scores = (
        jnp.einsum(
            "scqhd,sckhd->scqhk", cross_query, cross_keys, preferred_element_type=jnp.float32
        )
        * score_scale
    )
    masked = jnp.where(allowed, scores, NEGATIVE)
    row_peak = jnp.max(masked, axis=-1, keepdims=True)
    weights_exp = jnp.where(allowed, jnp.exp(masked - row_peak), 0.0)
    cross_total = jnp.sum(weights_exp, axis=-1, keepdims=True)
    cross_prob = weights_exp / jnp.where(cross_total > 0.0, cross_total, 1.0)
    cross_low = cross_prob.astype(jnp.bfloat16)
    windows = (
        jnp.einsum(
            "scqhk,sckhd->scqhd", cross_low, cross_values, preferred_element_type=jnp.float32
        )
        .astype(jnp.bfloat16)
        .reshape(seq_count, tok_rows, D)
    )
    after_rows = from_behind(windows[:, :1, :], "seq", -1)
    cross_rows = jnp.concatenate([windows[:, 1:, :], after_rows], axis=1).reshape(all_rows, D)
    after_cross = after_attn + matmul(cross_rows, cross_weight)
    normed_three = norm_rows(after_cross, mlp_gain, mlp_shift).astype(jnp.bfloat16)
    up_value = matmul(normed_three, up_weight)
    activated_full, gelu_pull = jax.vjp(gelu_exact, up_value)
    activated = activated_full.astype(jnp.bfloat16)
    output = (
        (after_cross + matmul(activated, down_weight))
        .astype(jnp.bfloat16)
        .reshape(seq_count, tok_rows, D)
    )
    grad_rows = cotangent.reshape(all_rows, D)
    grad_down = matmul_rows(activated, grad_rows)
    grad_up_in = gelu_pull(matmul_back(grad_rows, down_weight))[0].astype(jnp.bfloat16)
    grad_up = matmul_rows(normed_three, grad_up_in)
    mlp_norm_pull = jax.vjp(norm_rows, after_cross, mlp_gain, mlp_shift)[1]
    grad_into_three, grad_mlp_gain, grad_mlp_shift = mlp_norm_pull(
        matmul_back(grad_up_in, up_weight)
    )
    grad_cross_res = grad_rows.astype(jnp.float32) + grad_into_three
    grad_cross_low = grad_cross_res.astype(jnp.bfloat16)
    grad_cross = matmul_rows(cross_rows, grad_cross_low)
    grad_cross_rows = (
        matmul_back(grad_cross_low, cross_weight)
        .astype(jnp.bfloat16)
        .reshape(seq_count, tok_rows, D)
    )
    from_before = from_behind(grad_cross_rows[:, -1:, :], "seq", 1)
    grad_windows = jnp.concatenate([from_before, grad_cross_rows[:, :-1, :]], axis=1).reshape(
        seq_count, group_count, GROUP, HEADS, HD
    )
    grad_prob = jnp.einsum(
        "scqhd,sckhd->scqhk", grad_windows, cross_values, preferred_element_type=jnp.float32
    )
    grad_scores = (
        cross_prob * (grad_prob - jnp.sum(cross_prob * grad_prob, axis=-1, keepdims=True))
    ).astype(jnp.bfloat16)
    query_grad_low = (
        (
            jnp.einsum(
                "scqhk,sckhd->scqhd", grad_scores, cross_keys, preferred_element_type=jnp.float32
            )
            * score_scale
        )
        .astype(jnp.bfloat16)
        .reshape(all_rows, D)
    )
    key_grad = (
        jnp.einsum(
            "scqhk,scqhd->sckhd", grad_scores, cross_query, preferred_element_type=jnp.float32
        )
        * score_scale
    )
    value_grad = jnp.einsum(
        "scqhk,scqhd->sckhd", cross_low, grad_windows, preferred_element_type=jnp.float32
    )
    memory_grad_low = (
        jnp.stack([key_grad, value_grad], axis=3)
        .astype(jnp.bfloat16)
        .reshape(seq_count * group_count * NEIGH * RET, 2 * D)
    )
    grad_memory = matmul_rows(neigh_rows, memory_grad_low)
    grad_neighbours = (
        matmul_back(memory_grad_low, memory_weight).astype(jnp.bfloat16).reshape(neighbours.shape)
    )
    grad_query = matmul_rows(shifted, query_grad_low)
    grad_shifted = matmul_back(query_grad_low, query_weight).reshape(seq_count, tok_rows, D)
    after_grads = from_behind(grad_shifted[:, :1, :], "seq", -1)
    grad_normed_two = jnp.concatenate([grad_shifted[:, 1:, :], after_grads], axis=1).reshape(
        all_rows, D
    )
    cross_norm_pull = jax.vjp(norm_rows, after_attn, cross_gain, cross_shift)[1]
    grad_into_two, grad_cross_gain, grad_cross_shift = cross_norm_pull(grad_normed_two)
    grad_attn_res = grad_cross_res + grad_into_two
    grad_attn_low = grad_attn_res.astype(jnp.bfloat16)
    grad_attn = matmul_rows(attn_low, grad_attn_low)
    grad_heads = (
        matmul_back(grad_attn_low, attn_weight)
        .astype(jnp.bfloat16)
        .reshape(seq_count, tok_rows, HEADS, HD)
    )
    delta = jnp.sum(grad_heads.astype(jnp.float32) * attn_full, axis=-1)
    keys_all, values_all = collect_keys(keys_own, values_own)
    query_grad = (
        query_grads(
            queries, grad_heads, delta, log_total, query_positions, query_last, keys_all, values_all
        )
        * score_scale
    )
    block_len = math.gcd(lax.axis_size("seq") * tok_rows, 512)

    def key_visit_block(step_index):
        key_start = step_index * block_len

        def key_compute(unused):
            key_block = lax.dynamic_slice_in_dim(keys_all, key_start, block_len, 1).reshape(
                seq_count, block_len, HEADS, HD
            )
            value_block = lax.dynamic_slice_in_dim(values_all, key_start, block_len, 1).reshape(
                seq_count, block_len, HEADS, HD
            )
            probability, grad_score = block_grads(
                queries,
                grad_heads,
                delta,
                log_total,
                query_positions,
                key_start,
                key_block,
                value_block,
            )
            value_part = jnp.einsum(
                "sthk,sthd->kshd",
                probability.astype(jnp.bfloat16),
                grad_heads,
                preferred_element_type=jnp.float32,
            ).reshape(block_len, seq_count, D)
            key_part = (
                jnp.einsum(
                    "sthk,sthd->kshd", grad_score, queries, preferred_element_type=jnp.float32
                )
                * score_scale
            ).reshape(block_len, seq_count, D)
            return jnp.concatenate([key_part, value_part], axis=2)

        return lax.cond(
            key_start <= query_last,
            key_compute,
            lambda unused: jnp.zeros((block_len, seq_count, 2 * D), jnp.float32),
            0,
        )

    key_terms = jnp.swapaxes(
        lax.psum_scatter(
            lax.map(
                key_visit_block,
                jnp.arange(lax.axis_size("seq") * tok_rows // block_len, dtype=jnp.int32),
            )
            .reshape(lax.axis_size("seq") * tok_rows, seq_count, 2 * D)
            .astype(jnp.bfloat16),
            "seq",
            scatter_dimension=0,
            tiled=True,
        ).astype(jnp.float32),
        0,
        1,
    )
    key_sums = key_terms[..., :D].reshape(seq_count, tok_rows, HEADS, HD)
    grad_values = key_terms[..., D:].reshape(seq_count, tok_rows, HEADS, HD)
    grad_keys = rotate(key_sums, query_positions, -1.0)
    grad_proj = (
        jnp.stack([rotate(query_grad, query_positions, -1.0), grad_keys, grad_values], axis=2)
        .astype(jnp.bfloat16)
        .reshape(all_rows, 3 * D)
    )
    grad_qkv = matmul_rows(normed_one, grad_proj)
    attn_norm_pull = jax.vjp(norm_rows, token_vals, attn_gain, attn_shift)[1]
    grad_into_one, grad_attn_gain, grad_attn_shift = attn_norm_pull(
        matmul_back(grad_proj, qkv_weight)
    )
    grad_tokens = (
        (grad_attn_res + grad_into_one).astype(jnp.bfloat16).reshape(seq_count, tok_rows, D)
    )
    shares = (
        lax.psum_scatter(
            grad_qkv.astype(jnp.bfloat16), "seq", scatter_dimension=0, tiled=True
        ).astype(jnp.float32),
        lax.psum_scatter(
            grad_attn.astype(jnp.bfloat16), "seq", scatter_dimension=0, tiled=True
        ).astype(jnp.float32),
        lax.psum_scatter(
            grad_query.astype(jnp.bfloat16), "seq", scatter_dimension=0, tiled=True
        ).astype(jnp.float32),
        lax.psum_scatter(
            grad_memory.astype(jnp.bfloat16), "seq", scatter_dimension=0, tiled=True
        ).astype(jnp.float32),
        lax.psum_scatter(
            grad_cross.astype(jnp.bfloat16), "seq", scatter_dimension=0, tiled=True
        ).astype(jnp.float32),
        lax.psum_scatter(
            grad_up.astype(jnp.bfloat16), "seq", scatter_dimension=0, tiled=True
        ).astype(jnp.float32),
        lax.psum_scatter(
            grad_down.astype(jnp.bfloat16), "seq", scatter_dimension=0, tiled=True
        ).astype(jnp.float32),
        lax.psum_scatter(
            grad_attn_gain.astype(jnp.bfloat16), "seq", scatter_dimension=0, tiled=True
        ).astype(jnp.float32),
        lax.psum_scatter(
            grad_attn_shift.astype(jnp.bfloat16), "seq", scatter_dimension=0, tiled=True
        ).astype(jnp.float32),
        lax.psum_scatter(
            grad_cross_gain.astype(jnp.bfloat16), "seq", scatter_dimension=0, tiled=True
        ).astype(jnp.float32),
        lax.psum_scatter(
            grad_cross_shift.astype(jnp.bfloat16), "seq", scatter_dimension=0, tiled=True
        ).astype(jnp.float32),
        lax.psum_scatter(
            grad_mlp_gain.astype(jnp.bfloat16), "seq", scatter_dimension=0, tiled=True
        ).astype(jnp.float32),
        lax.psum_scatter(
            grad_mlp_shift.astype(jnp.bfloat16), "seq", scatter_dimension=0, tiled=True
        ).astype(jnp.float32),
    )
    totals = (
        lax.psum(shares[0].astype(jnp.bfloat16), "batch").astype(jnp.float32),
        lax.psum(shares[1].astype(jnp.bfloat16), "batch").astype(jnp.float32),
        lax.psum(shares[2].astype(jnp.bfloat16), "batch").astype(jnp.float32),
        lax.psum(shares[3].astype(jnp.bfloat16), "batch").astype(jnp.float32),
        lax.psum(shares[4].astype(jnp.bfloat16), "batch").astype(jnp.float32),
        lax.psum(shares[5].astype(jnp.bfloat16), "batch").astype(jnp.float32),
        lax.psum(shares[6].astype(jnp.bfloat16), "batch").astype(jnp.float32),
        lax.psum(shares[7].astype(jnp.bfloat16), "batch").astype(jnp.float32),
        lax.psum(shares[8].astype(jnp.bfloat16), "batch").astype(jnp.float32),
        lax.psum(shares[9].astype(jnp.bfloat16), "batch").astype(jnp.float32),
        lax.psum(shares[10].astype(jnp.bfloat16), "batch").astype(jnp.float32),
        lax.psum(shares[11].astype(jnp.bfloat16), "batch").astype(jnp.float32),
        lax.psum(shares[12].astype(jnp.bfloat16), "batch").astype(jnp.float32),
    )
    return (
        output,
        grad_tokens,
        grad_neighbours,
        totals[0],
        totals[1],
        totals[2],
        totals[3],
        totals[4],
        totals[5],
        totals[6],
        totals[7],
        totals[8],
        totals[9],
        totals[10],
        totals[11],
        totals[12],
    )


def solution(mesh):
    return jax.shard_map(
        shards,
        mesh=mesh,
        in_specs=(
            P("batch", "seq", None),
            P("batch", "seq", None, None, None),
            P("batch", "seq", None),
            P(),
            P(),
            P(),
            P(),
            P(),
            P(),
            P(),
            P(),
            P(),
            P(),
            P(),
            P(),
            P(),
            P("batch", "seq", None),
        ),
        out_specs=(
            P("batch", "seq", None),
            P("batch", "seq", None),
            P("batch", "seq", None, None, None),
            P("seq", None),
            P("seq", None),
            P("seq", None),
            P("seq", None),
            P("seq", None),
            P("seq", None),
            P("seq", None),
            P("seq"),
            P("seq"),
            P("seq"),
            P("seq"),
            P("seq"),
            P("seq"),
        ),
        check_vma=False,
    )
```

profile of v0, /device:TPU:0, one launch (start us, length us, event | category | flops | bytes accessed | tf_op | source)
XLA Modules:
  0.0 1048.9 jit_solution(10899886349985287407)
XLA Ops:
  49.3 11.3 %reshape.504 = bf16[2,4,256,2,12,64]{2,1,0,5,4,3:T(4,128)(2,1)} reshape(bf16[2048,1536]{0,1:T(8,128)(2,1)} %copy.122) | data formatting | bytes 12582912 | tf_op jit(solution)/shard_map/reshape | solution.py:248
  69.9 24.4 %all-gather.5.cloned.1.call-done = bf16[2,2048,768]{1,2,0:T(8,128)(2,1)} async-done(((bf16[2,256,768]{1,2,0:T(8,128)(2,1)}), bf16[2,2048,768]{1,2,0:T(8,128)(2,1)}) %all-gather.5.cloned.1.call-update) | async-done | bytes 6291472 | tf_op jit(solution)/shard_map/all_gather | solution.py:226
  94.3 65.6 %all-gather.3.cloned.1.call-done = bf16[2,2048,768]{1,2,0:T(8,128)(2,1)} async-done(((bf16[2,256,768]{1,2,0:T(8,128)(2,1)}), bf16[2,2048,768]{1,2,0:T(8,128)(2,1)}) %all-gather.3.cloned.1.call-update) | async-done | bytes 6291472 | tf_op jit(solution)/shard_map/all_gather | solution.py:225
  161.2 12.5 %while.46 = (s32[]{:T(128)}, f32[2,256,12]{1,2,0:T(8,128)S(1)}, f32[2,256,12]{1,2,0:T(8,128)S(1)}, f32[2,256,12,64]{1,3,2,0:T(8,128)}, s32[]{:T(128)}, /*index=5...) while((s32[]{:T(128)}, f32[2,256,12]{1,2,0:T(8,128)S(1)}, ...), condition=%wide.region_7.8_spmd.clone, body=%wide.region_2.7_spmd.clone.sunk | while | flops 847131392 | bytes 67772840 | solution.py:119
  161.2 12.3 %conditional.9 = ((f32[2,256,12]{1,2,0:T(8,128)S(1)}, f32[2,256,12]{1,2,0:T(8,128)S(1)}, f32[2,256,12,64]{1,3,2,0:T(8,128)})) conditional(s32[]{:T(128)} %convert_element_type.435, (f32[2,256,12]{1,2,0:T(8,128)S(1)}, f32[2,256,12]{1,2,0:T(8,128)S(1)}, f32[2,256,12,64]{1,3,2,0:T(8,128)}) %tuple.160, (s32[]{:T(128)}, s32[]{:T(128)}, s32[]{:T(128)}, ...), branch_computations={%region_3.0_spmd, %region_4.6_spmd} | conditional | flops 847131392 | bytes 67771568 | solution.py:115
  215.0 10.8 %collective-permute-done.1 = bf16[2,1,768]{1,2,0:T(8,128)(2,1)} collective-permute-done((bf16[2,1,768]{1,2,0:T(8,128)(2,1)}, bf16[2,1,768]{1,2,0:T(8,128)(2,1)}, u32[]{:S(2)}, u32[]{:S(2)}) %collective-permute-start.1) | collective-permute-done | bytes 3104 | tf_op jit(solution)/shard_map/ppermute | solution.py:23
  238.7 18.0 %add_convert_fusion = (bf16[512,3072]{1,0:T(8,128)(2,1)S(1)}, f32[512,3072]{1,0:T(8,128)}) fusion(f32[512,3072]{1,0:T(8,128)S(1)} %fusion.113, bf16[512,768]{1,0:T(8,128)(2,1)S(1)} %bitcast.316, bf16[3072,768]{1,0:T(8,128)(2,1)S(1)} %bitcast.336), kind=kOutput, calls=%fused_computation.81 | convolution fusion | flops 2529165312 | bytes 21233664 | tf_op jit(solution)/shard_map/dot_general | solution.py:59
  334.7 78.3 %while.48 = (s32[]{:T(128)}, bf16[4,512,2,1536]{3,1,0,2:T(8,128)(2,1)}, s32[4]{0:T(128)S(1)}, s32[]{:T(128)}, bf16[2,2048,768]{1,2,0:T(8,128)(2,1)}, /*index=5*/...) while((s32[]{:T(128)}, ...), condition=%wide.region_27.28_spmd.clone, body=%wide.region_24.27_spmd.clone.sunk | while | flops 1650066176 | bytes 82264416 | solution.py:407
  336.4 33.3 %conditional.11 = (bf16[1,512,2,1536]{1,3,2,0:T(8,128)(2,1)}) conditional(s32[]{:T(128)} %convert_element_type.437, () %tuple.165, (s32[]{:T(128)}, s32[]{:T(128)}, bf16[2,2048,768]{1,2,0:T(8,128)(2,1)}, bf16[2,256,12,64]{1,3,2,0:T(8,128)(2,1)}, f32[2,256,12]{1,2,0:T(8,128)S(1)}, /*index=5*/bf16[2,2048,768]{1,2,0:T(8,128)(2,1)}, ...), branch_computations={%region_25.25_spmd, %region_26.26_spmd} | conditional | flops 1650066176 | bytes 69680232 | solution.py:398
  348.0 11.9 %fusion.46 = bf16[2,12,512,64]{2,3,1,0:T(8,128)(2,1)} fusion(bf16[2,256,12,64]{1,3,2,0:T(8,128)(2,1)} %get-tuple-element.465, f32[2,12,512,256]{3,2,1,0:T(8,128)} %fusion.124, f32[2,256,12]{1,2,0:T(8,128)S(1)} %get-tuple-element.469, f32[2,256,12]{1,2,0:T(8,128)S(1)} %get-tuple-element.466, pred[256,512]{0,1:T(8,128)(4,1)S(1)} %broadcast_compare_fusion.2, ...), kind=kOutput, calls=%fused_computation.54 | convolution fusion | flops 825753600 | bytes 17481728 | tf_op jit(solution)/shard_map/while/body/eval_jaxpr/cond/branch_1_fun/sthk,sthd->kshd/dot_general | solution.py:391
  423.3 11.1 %copy.145 = bf16[2,4,256,2,12,64]{2,1,0,5,4,3:T(4,128)(2,1)} copy(bf16[2,4,256,2,12,64]{2,5,4,1,0,3:T(8,128)(2,1)} %maximum_convert_fusion) | data formatting | bytes 12582912 | tf_op jit(solution)/shard_map/convert_element_type | solution.py:331
  434.4 11.1 %convert_element_type.299 = bf16[2048,1536]{0,1:T(8,128)(2,1)} reshape(bf16[2,4,256,2,12,64]{2,1,0,5,4,3:T(4,128)(2,1)} %copy.145) | data formatting | bytes 12582912 | tf_op jit(solution)/shard_map/convert_element_type | solution.py:331
  498.9 23.4 %while.47 = (s32[]{:T(128)}, f32[2,256,12,64]{1,3,2,0:T(8,128)}, s32[]{:T(128)}, bf16[2,2048,768]{1,2,0:T(8,128)(2,1)}, bf16[2,256,12,64]{1,3,2,0:T(8,128)(2,1)}...) while((s32[]{:T(128)}, f32[2,256,12,64]{1,3,2,0:T(8,128)}, ...), condition=%wide.region_23.24_spmd.clone, body=%wide.region_20.23_spmd.clone.sunk | while | flops 1227358976 | bytes 50651472 | solution.py:173
  498.9 23.1 %conditional.10 = (f32[2,256,12,64]{1,3,2,0:T(8,128)}) conditional(s32[]{:T(128)} %convert_element_type.436, f32[2,256,12,64]{1,3,2,0:T(8,128)} %get-tuple-element.1171, (s32[]{:T(128)}, bf16[2,2048,768]{1,2,0:T(8,128)(2,1)}, s32[]{:T(128)}, bf16[2,256,12,64]{1,3,2,0:T(8,128)(2,1)}, f32[2,256,12]{1,2,0:T(8,128)S(1)}, ...), branch_computations={%region_21.21_spmd, %region_22.22_spmd} | conditional | flops 1227358976 | bytes 50650224 | solution.py:171
  509.9 12.1 %bitcast_add_fusion.1 = f32[2,256,12,64]{1,3,2,0:T(8,128)} fusion(f32[2,256,12,64]{1,3,2,0:T(8,128)} %get-tuple-element.442, bf16[2,512,12,64]{1,3,2,0:T(8,128)(2,1)} %bitcast.297, f32[2,12,512,256]{3,2,1,0:T(8,128)} %fusion.123, f32[2,256,12]{1,2,0:T(8,128)S(1)} %get-tuple-element.450, f32[2,256,12]{1,2,0:T(8,128)S(1)} %get-tuple-element.447, ...), kind=kOutput, calls=%fused_computation.30 | convolution fusion | flops 824573952 | bytes 19841024 | tf_op jit(solution)/shard_map/while/body/eval_jaxpr/cond/branch_1_fun/sthk,skhd->sthd/dot_general | solution.py:167
  525.0 130.0 %reduce-scatter.11.cloned.1.call-done = bf16[256,2,1536]{2,0,1:T(8,128)(2,1)} async-done(((bf16[2048,2,1536]{2,0,1:T(8,128)(2,1)}), bf16[256,2,1536]{2,0,1:T(8,128)(2,1)}) %reduce-scatter.11.cloned.1.call-update) | async-done | bytes 1572880 | tf_op jit(solution)/shard_map/reduce_scatter | solution.py:406
  693.7 32.4 %reduce-scatter.19.cloned.1.call-done = bf16[96,768]{1,0:T(8,128)(2,1)} async-done(((bf16[768,768]{1,0:T(8,128)(2,1)}), bf16[96,768]{1,0:T(8,128)(2,1)}) %reduce-scatter.19.cloned.1.call-update) | async-done | bytes 147472 | tf_op jit(solution)/shard_map/reduce_scatter | solution.py:449
  726.0 33.5 %reduce-scatter.17.cloned.1.call-done = bf16[96,768]{1,0:T(8,128)(2,1)} async-done(((bf16[768,768]{1,0:T(8,128)(2,1)}), bf16[96,768]{1,0:T(8,128)(2,1)}) %reduce-scatter.17.cloned.1.call-update) | async-done | bytes 147472 | tf_op jit(solution)/shard_map/reduce_scatter | solution.py:443
  759.5 34.1 %reduce-scatter.15.cloned.1.call-done = bf16[96,768]{1,0:T(8,128)(2,1)} async-done(((bf16[768,768]{1,0:T(8,128)(2,1)}), bf16[96,768]{1,0:T(8,128)(2,1)}) %reduce-scatter.15.cloned.1.call-update) | async-done | bytes 147472 | tf_op jit(solution)/shard_map/reduce_scatter | solution.py:440
  793.6 55.5 %reduce-scatter.23.cloned.1.call-done = bf16[384,768]{1,0:T(8,128)(2,1)} async-done(((bf16[3072,768]{1,0:T(8,128)(2,1)}), bf16[384,768]{1,0:T(8,128)(2,1)}) %reduce-scatter.23.cloned.1.call-update) | async-done | bytes 589840 | tf_op jit(solution)/shard_map/reduce_scatter | solution.py:455
  849.2 55.7 %reduce-scatter.21.cloned.1.call-done = bf16[96,3072]{1,0:T(8,128)(2,1)} async-done(((bf16[768,3072]{1,0:T(8,128)(2,1)}), bf16[96,3072]{1,0:T(8,128)(2,1)}) %reduce-scatter.21.cloned.1.call-update) | async-done | bytes 589840 | tf_op jit(solution)/shard_map/reduce_scatter | solution.py:452
  904.8 44.4 %reduce-scatter.13.cloned.1.call-done = bf16[96,2304]{1,0:T(8,128)(2,1)} async-done(((bf16[768,2304]{1,0:T(8,128)(2,1)}), bf16[96,2304]{1,0:T(8,128)(2,1)}) %reduce-scatter.13.cloned.1.call-update) | async-done | bytes 442384 | tf_op jit(solution)/shard_map/reduce_scatter | solution.py:437
  965.2 27.3 %all-reduce.6 = (bf16[768]{0:T(1024)(128)(2,1)S(1)}, bf16[768]{0:T(1024)(128)(2,1)S(1)}, bf16[768]{0:T(1024)(128)(2,1)S(1)}, bf16[768]{0:T(1024)(128)(2,1)S(1)},...) all-reduce(bf16[768]{0:T(1024)(128)(2,1)S(1)} %get-tuple-element.75, ...), channel_id=10, replica_groups=mesh['batch'=4,'seq'=8] {'seq'}, use_global_device_ids=true, to_apply=%region_46.47.clone | all-reduce | flops 4608 | bytes 18432
  1009.6 20.3 %all-reduce.11.cloned.1.call-done = (bf16[96,1536]{0,1:T(8,128)(2,1)}, bf16[96,2304]{1,0:T(8,128)(2,1)}, bf16[96,768]{1,0:T(8,128)(2,1)}, bf16[96,768]{1,0:T(8,1...) async-done(((bf16[96,1536]{0,1:T(8,128)(2,1)}, bf16[96,2304]{1,0:T(8,128)(2,1)}, bf16[96,768]{1,0:T(8,128)(2,1)}, ...) | async-done | bytes 2359312 | tf_op jit(solution)/shard_map/psum | solution.py:481
  (380 shorter events, 425.4 us)
Async XLA Ops:
  7.2 24.7 %copy-start = (bf16[2,4,2,128,768]{4,3,2,1,0:T(8,128)(2,1)S(1)}, bf16[2,4,2,128,768]{4,3,2,1,0:T(8,128)(2,1)}, u32[]{:S(2)}) copy-start(bf16[2,4,2,128,768]{4,3,2,1,0:T(8,128)(2,1)} %param.30) | copy-start | bytes 9437188
  7.2 87.1 %all-gather.5.cloned.1.call-start = ((), (), s32[]{:S(2)}) async-start(), calls=%async_computation.9 | async-start | bytes 7077888 | tf_op jit(solution)/shard_map/all_gather | solution.py:226
  26.3 133.6 %all-gather.3.cloned.1.call-start = ((), (), s32[]{:S(2)}) async-start(), calls=%async_computation.8 | async-start | bytes 7077888 | tf_op jit(solution)/shard_map/all_gather | solution.py:225
  31.7 623.3 %reduce-scatter.11.cloned.1.call-start = ((), (), s32[]{:S(2)}) async-start(), calls=%async_computation.10 | async-start | bytes 14155776 | tf_op jit(solution)/shard_map/reduce_scatter | solution.py:406
  49.3 13.2 %copy-start.59 = (s32[2,4,2]{1,2,0:T(2,128)S(1)}, s32[2,4,2]{1,2,0:T(2,128)}, u32[]{:S(2)}) copy-start(s32[2,4,2]{1,2,0:T(2,128)} %param.31) | copy-start | bytes 196
  180.8 3.0 collective-permute-start
  211.8 14.0 %collective-permute-start.1 = (bf16[2,1,768]{1,2,0:T(8,128)(2,1)}, bf16[2,1,768]{1,2,0:T(8,128)(2,1)}, u32[]{:S(2)}, u32[]{:S(2)}) collective-permute-start(bf16[2,1,768]{1,2,0:T(8,128)(2,1)} %slice.105), channel_id=1, source_target_pairs={{1,0},{2,1},{3,2},{4,3},{5,4},{6,5},{7,6},{9,8},{10,9},{11,10},{12... | collective-permute-start | bytes 9224 | tf_op jit(solution)/shard_map/ppermute | solution.py:23
  233.2 26.9 %copy-start.11 = (f32[512,768]{1,0:T(8,128)}, f32[512,768]{1,0:T(8,128)S(1)}, u32[]{:S(2)}) copy-start(f32[512,768]{1,0:T(8,128)S(1)} %get-tuple-element.884) | copy-start | bytes 4718596
  233.3 26.9 %copy-start.47 = (f32[512]{0:T(512)}, f32[512]{0:T(512)S(1)}, u32[]{:S(2)}) copy-start(f32[512]{0:T(512)S(1)} %broadcast_multiply_fusion.2) | copy-start | bytes 6148
  233.6 26.6 %copy-start.50 = (f32[512]{0:T(512)}, f32[512]{0:T(512)S(1)}, u32[]{:S(2)}) copy-start(f32[512]{0:T(512)S(1)} %fusion.106) | copy-start | bytes 6148
  233.6 23.0 %slice-start = ((s8[4718592]{0:T(1024)(128)(4,1)}), s8[4194304]{0:T(1024)(128)(4,1)S(1)}, s32[]{:S(2)}) async-start(s8[4718592]{0:T(1024)(128)(4,1)} %bitcast.333), calls=%async_computation.19 | async-start | bytes 8388608
  238.6 18.0 %copy-start.19 = (f32[512,3072]{1,0:T(8,128)}, f32[512,3072]{1,0:T(8,128)S(1)}, u32[]{:S(2)}) copy-start(f32[512,3072]{1,0:T(8,128)S(1)} %fusion.113) | copy-start | bytes 18874372
  238.6 18.0 %slice-start.1 = ((s8[4718592]{0:T(1024)(128)(4,1)}), s8[524288]{0:T(1024)(128)(4,1)S(1)}, s32[]{:S(2)}) async-start(s8[4718592]{0:T(1024)(128)(4,1)} %bitcast.333), calls=%async_computation.20 | async-start | bytes 1048576
  264.2 11.6 %collective-permute-start.2 = (bf16[2,1,768]{1,2,0:T(8,128)(2,1)}, bf16[2,1,768]{1,2,0:T(8,128)(2,1)}, u32[]{:S(2)}, u32[]{:S(2)}) collective-permute-start(bf16[2,1,768]{1,2,0:T(8,128)(2,1)} %copy.162), channel_id=1, source_target_pairs={{0,1},{1,2},{2,3},{3,4},{4,5},{5,6},{6,7},{8,9},{9,10},{10,11},{11... | collective-permute-start | bytes 9224 | tf_op jit(solution)/shard_map/ppermute | solution.py:23
  305.0 13.8 %copy-start.6 = (f32[512,768]{1,0:T(8,128)S(1)}, f32[512,768]{1,0:T(8,128)}, u32[]{:S(2)}) copy-start(f32[512,768]{1,0:T(8,128)} %copy-done.5) | copy-start | bytes 4718596
  305.0 13.1 %collective-permute-start.3 = (f32[2,1,768]{2,1,0:T(1,128)S(1)}, f32[2,1,768]{2,1,0:T(1,128)S(1)}, u32[]{:S(2)}, u32[]{:S(2)}) collective-permute-start(f32[2,1,768]{2,1,0:T(1,128)S(1)} %slice.109), channel_id=1, source_target_pairs={{1,0},{2,1},{3,2},{4,3},{5,4},{6,5},{7,6},{9,8},{10,9},{11,10},{12... | collective-permute-start | bytes 18440 | tf_op jit(solution)/shard_map/ppermute | solution.py:23
  413.0 278.8 %reduce-scatter.25.cloned.1.call-start = ((), (), s32[]{:S(2)}) async-start(), calls=%async_computation.17 | async-start | bytes 2654208
  458.9 267.2 %reduce-scatter.19.cloned.1.call-start = ((), (), s32[]{:S(2)}) async-start(), calls=%async_computation.14 | async-start | bytes 1327104 | tf_op jit(solution)/shard_map/reduce_scatter | solution.py:449
  462.2 297.4 %reduce-scatter.17.cloned.1.call-start = ((), (), s32[]{:S(2)}) async-start(), calls=%async_computation.13 | async-start | bytes 1327104 | tf_op jit(solution)/shard_map/reduce_scatter | solution.py:443
  473.2 320.4 %reduce-scatter.15.cloned.1.call-start = ((), (), s32[]{:S(2)}) async-start(), calls=%async_computation.12 | async-start | bytes 1327104 | tf_op jit(solution)/shard_map/reduce_scatter | solution.py:440
  476.7 372.4 %reduce-scatter.23.cloned.1.call-start = ((), (), s32[]{:S(2)}) async-start(), calls=%async_computation.16 | async-start | bytes 5308416 | tf_op jit(solution)/shard_map/reduce_scatter | solution.py:455
  489.0 415.8 %reduce-scatter.21.cloned.1.call-start = ((), (), s32[]{:S(2)}) async-start(), calls=%async_computation.15 | async-start | bytes 5308416 | tf_op jit(solution)/shard_map/reduce_scatter | solution.py:452
  497.1 452.1 %reduce-scatter.13.cloned.1.call-start = ((), (), s32[]{:S(2)}) async-start(), calls=%async_computation.11 | async-start | bytes 3981312 | tf_op jit(solution)/shard_map/reduce_scatter | solution.py:437
  675.5 354.4 %all-reduce.11.cloned.1.call-start = ((), (), s32[]{:S(2)}) async-start(), calls=%async_computation.18 | async-start | bytes 4915200 | tf_op jit(solution)/shard_map/psum | solution.py:481
  (64 other events, 218.8 us)
Sparse Core Ops, SparseCore 0:
  26.4 67.8 all-gather.4
  96.5 63.3 all-gather.2
  413.1 241.8 reduce-scatter.10
  657.2 34.5 reduce-scatter.24
  693.9 32.0 reduce-scatter.18
  728.8 30.7 reduce-scatter.16
  762.4 31.1 reduce-scatter.14
  795.9 53.1 reduce-scatter.22
  851.5 53.3 reduce-scatter.20
  907.0 42.1 reduce-scatter.12
  954.2 75.6 all-reduce.10
where the time goes:
time: 1060 us; the launch traced here: 1050 us
  waiting for transfers between devices  526 us (50%)
  local copies, waits for them, and re-layouts  198 us (19%)
  matrix products  178 us (17%)
  other arithmetic  74.4 us (7%)
  blocking collectives  37.4 us (4%)
  starting transfers between devices  15.8 us (1%)
  between operations  15.8 us (1%)
    reduce_scatter x1, waiting for transfers between devices, shards(): lax.psum_scatter(lax.map(key_visit_block, jnp.arange(lax.axis_size('seq')...  130 us
    all_gather x1, waiting for transfers between devices, shards(): lax.all_gather(keys_own, 'seq', axis=1, tiled=True)  65.6 us
    reduce_scatter x1, waiting for transfers between devices, shards(): lax.psum_scatter(grad_up.astype(jnp.bfloat16), 'seq', scatter_dimension=0...  55.7 us
    reduce_scatter x1, waiting for transfers between devices, shards(): lax.psum_scatter(grad_down.astype(jnp.bfloat16), 'seq', scatter_dimension...  55.5 us
    reduce_scatter x1, waiting for transfers between devices, shards(): lax.psum_scatter(grad_qkv.astype(jnp.bfloat16), 'seq', scatter_dimension=...  44.4 us
    dot_general x7, matrix products, matmul_back(): lax.dot_general(left, right, (((1,), (1,)), ((), ())), preferred_element_...  40.9 us
    unnamed x151, local copies, waits for them, and re-layouts  35.9 us
    dot_general x7, matrix products, matmul_rows(): lax.dot_general(left, right, (((0,), (0,)), ((), ())), preferred_element_...  34.5 us
  transfers between devices with their start and end apart: 15, of which 14 were waited for; matrix products, arithmetic and copies ran while one was open for 20% of the time, Pallas kernels for 0%

commit v1 on v0

v1 whole, which is shorter than its diff:
```python
import math

import jax
import jax.numpy as jnp
import numpy as np
from jax import lax
from jax.experimental import pallas as pl
from jax.experimental.pallas import tpu as pltpu
from jax.sharding import Mesh
from jax.sharding import PartitionSpec as P

D = 768
HEADS = 12
HD = 64
FF = 3072
GROUP = 64
NEIGH = 2
RET = 128
PAIR = 128
BLK = 256
GROUPS = 4

EPSILON = 1e-05
NEGATIVE = -1e30
SCALE = 1.0 / math.sqrt(HD)
LOG2E = math.log2(math.e)
VMEM_LIMIT = 56 * 1024 * 1024

F32 = jnp.float32
BF16 = jnp.bfloat16


def params(limit=VMEM_LIMIT):
    return pltpu.CompilerParams(vmem_limit_bytes=limit)


def dot(left, right):
    return jnp.dot(left, right, preferred_element_type=F32)


def dot_nt(left, right):
    return lax.dot_general(left, right, (((1,), (1,)), ((), ())), preferred_element_type=F32)


def dot_tn(left, right):
    return lax.dot_general(left, right, (((0,), (0,)), ((), ())), preferred_element_type=F32)


def flip(value):
    return jnp.transpose(value.astype(F32))


def rope_tables(length):
    half = HD // 2
    frequency = np.float32(10000.0) ** (-np.arange(half, dtype=np.float32) * np.float32(2.0) / np.float32(HD))
    angles = np.arange(length, dtype=np.float32)[:, None] * frequency[None, :].astype(np.float32)
    cosine, sine = np.cos(angles).astype(np.float32), np.sin(angles).astype(np.float32)
    return (
        np.concatenate([cosine] * 4, axis=1),
        np.concatenate([-sine, sine] * 2, axis=1),
    )


def lanes(rows):
    return lax.broadcasted_iota(jnp.int32, (rows, PAIR), 1)


def turn(tile, cosine, sine):
    rows = tile.shape[0]
    first = (lanes(rows) % HD) < HD // 2
    swapped = jnp.where(first, pltpu.roll(tile, PAIR - HD // 2, 1), pltpu.roll(tile, HD // 2, 1))
    return tile * cosine + swapped * sine


def swap_heads(tile):
    return pltpu.roll(tile, HD, 1)


def norm_stats(values):
    mean = jnp.mean(values, axis=-1, keepdims=True)
    centred = values - mean
    inverse = lax.rsqrt(jnp.mean(centred * centred, axis=-1, keepdims=True) + EPSILON)
    return centred * inverse, inverse


def norm_back(normed, inverse, gain, grad):
    scaled = grad * gain
    return inverse * (
        scaled
        - jnp.mean(scaled, axis=-1, keepdims=True)
        - normed * jnp.mean(scaled * normed, axis=-1, keepdims=True)
    )


def const(shape):
    rank = len(shape)
    return pl.BlockSpec(shape, lambda *ids: (0,) * rank)


def qkv_body(place, tok, gain, shift, weight, cosine, sine, first, second):
    rows = tok.shape[1]
    half = rows // 2
    normed, _ = norm_stats(tok[0].astype(F32))
    row = (normed * gain[...] + shift[...]).astype(BF16)
    out = dot(row, weight[...])
    cos, sin = cosine[...], sine[...]
    low = lanes(rows) < HD
    queries = [turn(out[:, i * PAIR : (i + 1) * PAIR], cos, sin) for i in range(6)]
    keys = [turn(out[:, D + i * PAIR : D + (i + 1) * PAIR], cos, sin) for i in range(6)]
    values = [out[:, 2 * D + i * PAIR : 2 * D + (i + 1) * PAIR] for i in range(6)]
    for g in range(GROUPS):
        first[g, 0, 0:rows] = queries[g].astype(BF16)
        first[g, 0, rows : 2 * rows] = keys[g].astype(BF16)
        first[g, 0, 2 * rows : 3 * rows] = values[g].astype(BF16)
        tile = GROUPS + g // 2
        key, value, query = keys[tile], values[tile], queries[tile]
        if g % 2 == 0:
            both = jnp.where(low, key, swap_heads(value))
            packed = jnp.where(low[:half], query[:half], swap_heads(query[half:]))
        else:
            both = jnp.where(low, swap_heads(key), value)
            packed = jnp.where(low[:half], swap_heads(query[:half]), query[half:])
        second[g, 0, 0:rows] = both.astype(BF16)
        second[g, 0, rows : rows + half] = packed.astype(BF16)


def qkv_call(place, tokens, gain, shift, weight, cosine, sine):
    seqs, rows, _ = tokens.shape
    return pl.pallas_call(
        qkv_body,
        grid_spec=pltpu.PrefetchScalarGridSpec(
            num_scalar_prefetch=1,
            grid=(seqs,),
            in_specs=[
                pl.BlockSpec((1, rows, D), lambda s, place: (s, 0, 0)),
                const((1, D)),
                const((1, D)),
                const((D, 3 * D)),
                pl.BlockSpec((rows, PAIR), lambda s, place: (place[0], 0)),
                pl.BlockSpec((rows, PAIR), lambda s, place: (place[0], 0)),
            ],
            out_specs=[
                pl.BlockSpec((GROUPS, 1, 3 * rows, PAIR), lambda s, place: (0, s, 0, 0)),
                pl.BlockSpec((GROUPS, 1, 3 * rows // 2, PAIR), lambda s, place: (0, s, 0, 0)),
            ],
        ),
        out_shape=[
            jax.ShapeDtypeStruct((GROUPS, seqs, 3 * rows, PAIR), BF16),
            jax.ShapeDtypeStruct((GROUPS, seqs, 3 * rows // 2, PAIR), BF16),
        ],
        compiler_params=params(),
        name="qkv",
    )(place, tokens, gain, shift, weight, cosine, sine)


def unpack_half(packed, rows):
    peers = packed.shape[0]
    wide = packed.astype(F32).reshape(peers * rows // 2, PAIR)
    low = lanes(peers * rows // 2) < HD
    top = jnp.where(low, wide, 0.0).reshape(peers, rows // 2, PAIR)
    bottom = jnp.where(low, swap_heads(wide), 0.0).reshape(peers, rows // 2, PAIR)
    return jnp.concatenate([top, bottom], axis=1).reshape(peers * rows, PAIR).astype(BF16)


def pack_half(tile, rows):
    blocks = tile.shape[0] // rows
    cut = tile.reshape(blocks, rows, PAIR)
    top = cut[:, : rows // 2].reshape(blocks * rows // 2, PAIR)
    bottom = cut[:, rows // 2 :].reshape(blocks * rows // 2, PAIR)
    return (top + swap_heads(bottom)).reshape(blocks, rows // 2, PAIR)


def causal():
    key = lax.broadcasted_iota(jnp.int32, (BLK, BLK), 0)
    query = lax.broadcasted_iota(jnp.int32, (BLK, BLK), 1)
    return key <= query


def head_masks(tile_t):
    upper = lax.broadcasted_iota(jnp.int32, tile_t.shape, 0) < HD
    return jnp.where(upper, tile_t, 0.0).astype(BF16), jnp.where(upper, 0.0, tile_t).astype(BF16)


def softmax_sweep(i, heads, key_at, value_t_at):
    c = SCALE * LOG2E

    def visit(j, carry, masked):
        keys = key_at(j)
        values_t = value_t_at(j)
        out = []
        for (query_t, at), (top, total, acc) in zip(heads, carry):
            s = dot(keys, query_t) * c
            if masked:
                s = jnp.where(causal(), s, NEGATIVE)
            peak = jnp.maximum(top, jnp.max(s, axis=0, keepdims=True))
            p = jnp.exp2(s - peak)
            fade = jnp.exp2(top - peak)
            out.append(
                (
                    peak,
                    total * fade + jnp.sum(p, axis=0, keepdims=True),
                    acc * fade + dot(values_t[at : at + HD], p.astype(BF16)),
                )
            )
        return tuple(out)

    start = tuple(
        (
            jnp.full((1, BLK), NEGATIVE, F32),
            jnp.zeros((1, BLK), F32),
            jnp.zeros((HD, BLK), F32),
        )
        for _ in heads
    )
    carry = lax.fori_loop(0, i, lambda j, carry: visit(j, carry, False), start)
    carry = visit(i, carry, True)
    return [(acc / total, top + jnp.log2(total)) for top, total, acc in carry]


def pair_forward_body(rows, peers, recv, out, out_t, lse, keys, values_t):
    i = pl.program_id(0)
    blocks = peers * rows // BLK

    @pl.when(i == 0)
    def _():
        keys[...] = recv[:, rows : 2 * rows].reshape(blocks, BLK, PAIR)
        values = recv[:, 2 * rows : 3 * rows].reshape(blocks, BLK, PAIR)
        for b in range(blocks):
            values_t[b] = flip(values[b]).astype(BF16)

    if rows >= BLK:
        query = recv[i, 0:BLK]
    else:
        query = recv[pl.ds(i * (BLK // rows), BLK // rows), 0:rows].reshape(BLK, PAIR)
    low, high = head_masks(flip(query))
    heads = softmax_sweep(
        i, [(low, 0), (high, HD)], lambda j: keys[j], lambda j: values_t[j]
    )
    o_t = jnp.concatenate([heads[0][0], heads[1][0]], axis=0)
    out_t[...] = o_t
    lse[0, 0:1] = heads[0][1]
    lse[0, 1:2] = heads[1][1]
    out[...] = jnp.transpose(o_t).astype(BF16)


def pair_forward(recv):
    peers, rows = recv.shape[0], recv.shape[1] // 3
    length = peers * rows
    blocks = length // BLK
    return pl.pallas_call(
        lambda *refs: pair_forward_body(rows, peers, *refs),
        grid=(blocks,),
        in_specs=[const(recv.shape)],
        out_specs=[
            pl.BlockSpec((BLK, PAIR), lambda i: (i, 0)),
            pl.BlockSpec((PAIR, BLK), lambda i: (0, i)),
            pl.BlockSpec((1, 8, BLK), lambda i: (i, 0, 0)),
        ],
        out_shape=[
            jax.ShapeDtypeStruct((length, PAIR), BF16),
            jax.ShapeDtypeStruct((PAIR, length), F32),
            jax.ShapeDtypeStruct((blocks, 8, BLK), F32),
        ],
        scratch_shapes=[
            pltpu.VMEM((blocks, BLK, PAIR), BF16),
            pltpu.VMEM((blocks, PAIR, BLK), BF16),
        ],
        compiler_params=params(),
        name="attend_pair",
    )(recv)


def single_forward_body(rows, peers, recv, out, out_t, lse, keys, values_t, queries):
    i = pl.program_id(0)
    blocks = peers * rows // BLK

    @pl.when(i == 0)
    def _():
        both = recv[:, 0:rows].reshape(blocks, BLK, PAIR)
        keys[...] = both
        for b in range(blocks):
            values_t[b] = flip(both[b]).astype(BF16)
        queries[...] = unpack_half(recv[:, rows : rows + rows // 2], rows).reshape(blocks, BLK, PAIR)

    query_t = flip(queries[i]).astype(BF16)
    ((o_t, total),) = softmax_sweep(
        i, [(query_t, HD)], lambda j: keys[j], lambda j: values_t[j]
    )
    out_t[...] = o_t
    lse[0, 0:1] = total
    tile = jnp.transpose(jnp.concatenate([o_t, jnp.zeros_like(o_t)], axis=0))
    out[...] = pack_half(tile, rows).astype(BF16)


def single_forward(recv):
    peers, rows = recv.shape[0], recv.shape[1] * 2 // 3
    length = peers * rows
    blocks = length // BLK
    per = BLK // rows
    return pl.pallas_call(
        lambda *refs: single_forward_body(rows, peers, *refs),
        grid=(blocks,),
        in_specs=[const(recv.shape)],
        out_specs=[
            pl.BlockSpec((per, rows // 2, PAIR), lambda i: (i, 0, 0)),
            pl.BlockSpec((HD, BLK), lambda i: (0, i)),
            pl.BlockSpec((1, 8, BLK), lambda i: (i, 0, 0)),
        ],
        out_shape=[
            jax.ShapeDtypeStruct((peers, rows // 2, PAIR), BF16),
            jax.ShapeDtypeStruct((HD, length), F32),
            jax.ShapeDtypeStruct((blocks, 8, BLK), F32),
        ],
        scratch_shapes=[
            pltpu.VMEM((blocks, BLK, PAIR), BF16),
            pltpu.VMEM((blocks, PAIR, BLK), BF16),
            pltpu.VMEM((blocks, BLK, PAIR), BF16),
        ],
        compiler_params=params(),
        name="attend_single",
    )(recv)


def unturn_t(part_t, cosine_t, sine_t):
    first, second = part_t[: HD // 2], part_t[HD // 2 :]
    return jnp.concatenate(
        [first * cosine_t + second * sine_t, second * cosine_t - first * sine_t], axis=0
    )


def grads_sweep(i, heads, key_at, value_at, key_t_at, add):
    c = SCALE * LOG2E

    def visit(j, carry, masked):
        keys, values, keys_t = key_at(j), value_at(j), key_t_at(j)
        ps, dss, out = [], [], []
        for (query_t, grad_t, lse, delta, at), dq in zip(heads, carry):
            p = jnp.exp2(dot(keys, query_t) * c - lse)
            if masked:
                p = jnp.where(causal(), p, 0.0)
            ds = (p * (dot(values, grad_t) - delta)).astype(BF16)
            ps.append(p.astype(BF16))
            dss.append(ds)
            out.append(dq + dot(keys_t[at : at + HD], ds))
        add(j, ps, dss)
        return tuple(out)

    start = tuple(jnp.zeros((HD, BLK), F32) for _ in heads)
    carry = lax.fori_loop(0, i, lambda j, carry: visit(j, carry, False), start)
    return visit(i, carry, True)


def pair_backward_body(
    rows, peers, recv, grad, out_t, lse, cos_t, sin_t, cosine, sine, out, keys, values, keys_t, dk, dv
):
    i = pl.program_id(0)
    blocks = peers * rows // BLK
    per = BLK // rows

    @pl.when(i == 0)
    def _():
        keys[...] = recv[:, rows : 2 * rows].reshape(blocks, BLK, PAIR)
        values[...] = recv[:, 2 * rows : 3 * rows].reshape(blocks, BLK, PAIR)
        for b in range(blocks):
            keys_t[b] = flip(keys[b]).astype(BF16)
        dk[...] = jnp.zeros_like(dk)
        dv[...] = jnp.zeros_like(dv)

    query = recv[pl.ds(i * per, per), 0:rows].reshape(BLK, PAIR)
    do = grad[pl.ds(i * per, per), 0:rows].reshape(BLK, PAIR)
    q_low, q_high = head_masks(flip(query))
    do_t = flip(do)
    do_low, do_high = head_masks(do_t)
    product = do_t * out_t[...]
    low = lanes(BLK) < HD
    wide_q, wide_do = query.astype(F32), do.astype(F32)
    q_rows = jnp.concatenate(
        [jnp.where(low, wide_q, 0.0), jnp.where(low, 0.0, wide_q)], axis=0
    ).astype(BF16)
    do_rows = jnp.concatenate(
        [jnp.where(low, wide_do, 0.0), jnp.where(low, 0.0, wide_do)], axis=0
    ).astype(BF16)

    def add(j, ps, dss):
        dv[j] += dot(jnp.concatenate(ps, axis=1), do_rows)
        dk[j] += dot(jnp.concatenate(dss, axis=1), q_rows)

    heads = [
        (q_low, do_low, lse[0, 0:1], jnp.sum(product[:HD], axis=0, keepdims=True), 0),
        (q_high, do_high, lse[0, 1:2], jnp.sum(product[HD:], axis=0, keepdims=True), HD),
    ]
    dqs = grads_sweep(
        i, heads, lambda j: keys[j], lambda j: values[j], lambda j: keys_t[j], add
    )
    cos, sin = cos_t[...], sin_t[...]
    dq = jnp.concatenate([unturn_t(part * SCALE, cos, sin) for part in dqs], axis=0)
    out[pl.ds(i * per, per), 0:rows] = jnp.transpose(dq).reshape(per, rows, PAIR).astype(BF16)

    @pl.when(i == blocks - 1)
    def _():
        for b in range(blocks):
            at = pl.ds(b * BLK, BLK)
            back = turn(dk[b] * SCALE, cosine[at], -sine[at])
            out[b * per : (b + 1) * per, rows : 2 * rows] = back.reshape(per, rows, PAIR).astype(BF16)
            out[b * per : (b + 1) * per, 2 * rows : 3 * rows] = (
                dv[b].reshape(per, rows, PAIR).astype(BF16)
            )


def pair_backward(recv, grad, out_t, lse, cos_t, sin_t, cosine, sine):
    peers, rows = recv.shape[0], recv.shape[1] // 3
    length = peers * rows
    blocks = length // BLK
    return pl.pallas_call(
        lambda *refs: pair_backward_body(rows, peers, *refs),
        grid=(blocks,),
        in_specs=[
            const(recv.shape),
            const(grad.shape),
            pl.BlockSpec((PAIR, BLK), lambda i: (0, i)),
            pl.BlockSpec((1, 8, BLK), lambda i: (i, 0, 0)),
            pl.BlockSpec((HD // 2, BLK), lambda i: (0, i)),
            pl.BlockSpec((HD // 2, BLK), lambda i: (0, i)),
            const(cosine.shape),
            const(sine.shape),
        ],
        out_specs=const(recv.shape),
        out_shape=jax.ShapeDtypeStruct(recv.shape, BF16),
        scratch_shapes=[
            pltpu.VMEM((blocks, BLK, PAIR), BF16),
            pltpu.VMEM((blocks, BLK, PAIR), BF16),
            pltpu.VMEM((blocks, PAIR, BLK), BF16),
            pltpu.VMEM((blocks, BLK, PAIR), F32),
            pltpu.VMEM((blocks, BLK, PAIR), F32),
        ],
        compiler_params=params(),
        name="attend_pair_grads",
    )(recv, grad, out_t, lse, cos_t, sin_t, cosine, sine)


def single_backward_body(
    rows,
    peers,
    recv,
    grad,
    out_t,
    lse,
    cos_t,
    sin_t,
    cosine,
    sine,
    out,
    both,
    both_t,
    queries,
    grads,
    dboth,
):
    i = pl.program_id(0)
    blocks = peers * rows // BLK
    per = BLK // rows
    half = rows // 2

    @pl.when(i == 0)
    def _():
        both[...] = recv[:, 0:rows].reshape(blocks, BLK, PAIR)
        for b in range(blocks):
            both_t[b] = flip(both[b]).astype(BF16)
        queries[...] = unpack_half(recv[:, rows : rows + half], rows).reshape(blocks, BLK, PAIR)
        grads[...] = unpack_half(grad[...], rows).reshape(blocks, BLK, PAIR)
        dboth[...] = jnp.zeros_like(dboth)

    wide_q, wide_do = queries[i].astype(F32), grads[i].astype(F32)
    q_t = jnp.transpose(wide_q).astype(BF16)
    shifted = swap_heads(wide_do)
    do_t = jnp.transpose(shifted)
    delta = jnp.sum(do_t[HD:] * out_t[...], axis=0, keepdims=True)
    sides = jnp.concatenate([wide_q, shifted], axis=0).astype(BF16)

    def add(j, ps, dss):
        dboth[j] += dot(jnp.concatenate([dss[0], ps[0]], axis=1), sides)

    (dq,) = grads_sweep(
        i,
        [(q_t, do_t.astype(BF16), lse[0, 0:1], delta, 0)],
        lambda j: both[j],
        lambda j: both[j],
        lambda j: both_t[j],
        add,
    )
    dq = unturn_t(dq * SCALE, cos_t[...], sin_t[...])
    tile = jnp.transpose(jnp.concatenate([dq, jnp.zeros_like(dq)], axis=0))
    out[pl.ds(i * per, per), rows : rows + half] = pack_half(tile, rows).astype(BF16)

    @pl.when(i == blocks - 1)
    def _():
        low = lanes(BLK) < HD
        for b in range(blocks):
            at = pl.ds(b * BLK, BLK)
            part = dboth[b]
            back = turn(part * SCALE, cosine[at], -sine[at])
            out[b * per : (b + 1) * per, 0:rows] = (
                jnp.where(low, back, part).reshape(per, rows, PAIR).astype(BF16)
            )


def single_backward(recv, grad, out_t, lse, cos_t, sin_t, cosine, sine):
    peers, rows = recv.shape[0], recv.shape[1] * 2 // 3
    length = peers * rows
    blocks = length // BLK
    return pl.pallas_call(
        lambda *refs: single_backward_body(rows, peers, *refs),
        grid=(blocks,),
        in_specs=[
            const(recv.shape),
            const(grad.shape),
            pl.BlockSpec((HD, BLK), lambda i: (0, i)),
            pl.BlockSpec((1, 8, BLK), lambda i: (i, 0, 0)),
            pl.BlockSpec((HD // 2, BLK), lambda i: (0, i)),
            pl.BlockSpec((HD // 2, BLK), lambda i: (0, i)),
            const(cosine.shape),
            const(sine.shape),
        ],
        out_specs=const(recv.shape),
        out_shape=jax.ShapeDtypeStruct(recv.shape, BF16),
        scratch_shapes=[
            pltpu.VMEM((blocks, BLK, PAIR), BF16),
            pltpu.VMEM((blocks, PAIR, BLK), BF16),
            pltpu.VMEM((blocks, BLK, PAIR), BF16),
            pltpu.VMEM((blocks, BLK, PAIR), BF16),
            pltpu.VMEM((blocks, BLK, PAIR), F32),
        ],
        compiler_params=params(),
        name="attend_single_grads",
    )(recv, grad, out_t, lse, cos_t, sin_t, cosine, sine)


def from_behind(value, axis, by):
    peers = lax.axis_size(axis)
    pairs = [(i, i + by) for i in range(peers) if 0 <= i + by < peers]
    return lax.ppermute(value, axis, pairs)


def norm_rows(values, gain_vec, shift_vec):
    row_mean = jnp.mean(values, axis=-1, keepdims=True)
    centred = values - row_mean
    variance = jnp.mean(centred * centred, axis=-1, keepdims=True)
    return centred * lax.rsqrt(variance + EPSILON) * gain_vec + shift_vec


def gelu_exact(values):
    return jax.nn.gelu(values, approximate=False)


SEQ = ("hg", "sq")
BATCH = ("by", "bx")


def swap_all(value):
    return lax.all_to_all(value, SEQ, 0, 0, tiled=True)


def heads_in(pair, single, seqs, rows):
    first = pair.reshape(GROUPS, seqs, rows, PAIR).transpose(1, 2, 0, 3).reshape(seqs, rows, GROUPS * PAIR)
    second = (
        single.reshape(GROUPS, seqs, rows // 2, 2, HD)
        .transpose(1, 3, 2, 0, 4)
        .reshape(seqs, rows, GROUPS * HD)
    )
    return jnp.concatenate([first, second], axis=-1)


def heads_out(value, seqs, rows):
    first = value[..., : GROUPS * PAIR].reshape(seqs, rows, GROUPS, PAIR).transpose(2, 0, 1, 3)
    second = (
        value[..., GROUPS * PAIR :]
        .reshape(seqs, 2, rows // 2, GROUPS, HD)
        .transpose(3, 0, 2, 1, 4)
        .reshape(GROUPS, seqs, rows // 2, PAIR)
    )
    return (
        first.reshape(GROUPS * seqs, rows, PAIR),
        second.reshape(GROUPS * seqs, rows // 2, PAIR),
    )


def add_up(value):
    kept = value.shape[3:]
    flat = value.reshape((value.shape[0] * value.shape[1],) + value.shape[2:])
    own = lax.psum_scatter(flat, BATCH + ("sq",), scatter_dimension=0, tiled=True)
    own = own.reshape((value.shape[2],) + kept)
    parts = lax.all_to_all(own, "hg", 0, 0, tiled=True)
    total = jnp.sum(parts.astype(F32), axis=0).astype(BF16)
    return lax.all_gather(total, BATCH, axis=0)


def by_columns(value, batch, sq):
    rows, cols = value.shape
    cut = value.astype(BF16).reshape(GROUPS, sq, rows // GROUPS // sq, batch, cols // batch)
    return cut.transpose(3, 1, 0, 2, 4)


def shards(
    tokens,
    neighbours,
    present,
    qkv_weight,
    attn_weight,
    query_weight,
    memory_weight,
    cross_weight,
    up_weight,
    down_weight,
    attn_gain,
    attn_shift,
    cross_gain,
    cross_shift,
    mlp_gain,
    mlp_shift,
    cotangent,
):
    seq_count, tok_rows = tokens.shape[:2]
    all_rows = seq_count * tok_rows
    group_count = neighbours.shape[1]
    peers = lax.axis_size(SEQ)
    batch = lax.axis_size(BATCH)
    length = peers * tok_rows
    here = lax.axis_index(SEQ)
    place = here.astype(jnp.int32).reshape(1)
    cos_np, sin_np = rope_tables(length)
    cosine, sine = jnp.asarray(cos_np), jnp.asarray(sin_np)
    cos_t = jnp.asarray(np.ascontiguousarray(cos_np[:, : HD // 2].T))
    sin_t = jnp.asarray(np.ascontiguousarray(sin_np[:, HD // 2 : HD].T))
    token_vals = tokens.astype(F32).reshape(all_rows, D)
    normed_one = norm_rows(token_vals, attn_gain, attn_shift).astype(BF16)
    first, second = qkv_call(
        place, tokens, attn_gain.reshape(1, D), attn_shift.reshape(1, D), qkv_weight, cosine, sine
    )
    first = swap_all(first.reshape(peers, 3 * tok_rows, PAIR))
    second = swap_all(second.reshape(peers, 3 * tok_rows // 2, PAIR))
    o_pair, o_pair_t, lse_pair = pair_forward(first)
    o_pair = swap_all(o_pair.reshape(peers, tok_rows, PAIR))
    o_single, o_single_t, lse_single = single_forward(second)
    o_single = swap_all(o_single)
    attn_low = heads_in(o_pair, o_single, seq_count, tok_rows).reshape(all_rows, D)
    score_scale = SCALE
    after_attn = token_vals + dot(attn_low, attn_weight)
    normed_two = (
        norm_rows(after_attn, cross_gain, cross_shift).astype(BF16).reshape(seq_count, tok_rows, D)
    )
    before_rows = from_behind(normed_two[:, -1:, :], SEQ, 1)
    shifted = jnp.concatenate([before_rows, normed_two[:, :-1, :]], axis=1).reshape(all_rows, D)
    cross_query = (
        dot(shifted, query_weight).astype(BF16).reshape(seq_count, group_count, GROUP, HEADS, HD)
    )
    neigh_rows = neighbours.reshape(seq_count * group_count * NEIGH * RET, D)
    memory = (
        dot(neigh_rows, memory_weight)
        .astype(BF16)
        .reshape(seq_count, group_count, NEIGH * RET, 2, HEADS, HD)
    )
    cross_keys = memory[:, :, :, 0]
    cross_values = memory[:, :, :, 1]
    allowed = jnp.repeat(present > 0, RET, axis=2)[:, :, None, None, :]
    scores = (
        jnp.einsum("scqhd,sckhd->scqhk", cross_query, cross_keys, preferred_element_type=F32)
        * score_scale
    )
    masked = jnp.where(allowed, scores, NEGATIVE)
    row_peak = jnp.max(masked, axis=-1, keepdims=True)
    weights_exp = jnp.where(allowed, jnp.exp(masked - row_peak), 0.0)
    cross_total = jnp.sum(weights_exp, axis=-1, keepdims=True)
    cross_prob = weights_exp / jnp.where(cross_total > 0.0, cross_total, 1.0)
    cross_low = cross_prob.astype(BF16)
    windows = (
        jnp.einsum("scqhk,sckhd->scqhd", cross_low, cross_values, preferred_element_type=F32)
        .astype(BF16)
        .reshape(seq_count, tok_rows, D)
    )
    after_rows = from_behind(windows[:, :1, :], SEQ, -1)
    cross_rows = jnp.concatenate([windows[:, 1:, :], after_rows], axis=1).reshape(all_rows, D)
    after_cross = after_attn + dot(cross_rows, cross_weight)
    normed_three = norm_rows(after_cross, mlp_gain, mlp_shift).astype(BF16)
    up_value = dot(normed_three, up_weight)
    activated_full, gelu_pull = jax.vjp(gelu_exact, up_value)
    activated = activated_full.astype(BF16)
    output = (after_cross + dot(activated, down_weight)).astype(BF16).reshape(seq_count, tok_rows, D)
    grad_rows = cotangent.reshape(all_rows, D)
    grad_down = dot_tn(activated, grad_rows)
    grad_up_in = gelu_pull(dot_nt(grad_rows, down_weight))[0].astype(BF16)
    grad_up = dot_tn(normed_three, grad_up_in)
    up_part = by_columns(grad_up, batch, seq_count)
    down_part = (
        grad_down.astype(BF16)
        .reshape(GROUPS, seq_count, batch, FF // peers // batch, D)
        .transpose(2, 1, 0, 3, 4)
    )
    feed = add_up(jnp.concatenate([up_part.reshape(down_part.shape), down_part], axis=3))
    mlp_norm_pull = jax.vjp(norm_rows, after_cross, mlp_gain, mlp_shift)[1]
    grad_into_three, grad_mlp_gain, grad_mlp_shift = mlp_norm_pull(dot_nt(grad_up_in, up_weight))
    grad_cross_res = grad_rows.astype(F32) + grad_into_three
    grad_cross_low = grad_cross_res.astype(BF16)
    grad_cross = dot_tn(cross_rows, grad_cross_low)
    grad_cross_rows = (
        dot_nt(grad_cross_low, cross_weight).astype(BF16).reshape(seq_count, tok_rows, D)
    )
    from_before = from_behind(grad_cross_rows[:, -1:, :], SEQ, 1)
    grad_windows = jnp.concatenate([from_before, grad_cross_rows[:, :-1, :]], axis=1).reshape(
        seq_count, group_count, GROUP, HEADS, HD
    )
    grad_prob = jnp.einsum(
        "scqhd,sckhd->scqhk", grad_windows, cross_values, preferred_element_type=F32
    )
    grad_scores = (
        cross_prob * (grad_prob - jnp.sum(cross_prob * grad_prob, axis=-1, keepdims=True))
    ).astype(BF16)
    query_grad_low = (
        (
            jnp.einsum("scqhk,sckhd->scqhd", grad_scores, cross_keys, preferred_element_type=F32)
            * score_scale
        )
        .astype(BF16)
        .reshape(all_rows, D)
    )
    key_grad = (
        jnp.einsum("scqhk,scqhd->sckhd", grad_scores, cross_query, preferred_element_type=F32)
        * score_scale
    )
    value_grad = jnp.einsum(
        "scqhk,scqhd->sckhd", cross_low, grad_windows, preferred_element_type=F32
    )
    memory_grad_low = (
        jnp.stack([key_grad, value_grad], axis=3)
        .astype(BF16)
        .reshape(seq_count * group_count * NEIGH * RET, 2 * D)
    )
    grad_memory = dot_tn(neigh_rows, memory_grad_low)
    grad_neighbours = dot_nt(memory_grad_low, memory_weight).astype(BF16).reshape(neighbours.shape)
    grad_query = dot_tn(shifted, query_grad_low)
    grad_shifted = dot_nt(query_grad_low, query_weight).reshape(seq_count, tok_rows, D)
    after_grads = from_behind(grad_shifted[:, :1, :], SEQ, -1)
    grad_normed_two = jnp.concatenate([grad_shifted[:, 1:, :], after_grads], axis=1).reshape(
        all_rows, D
    )
    cross_norm_pull = jax.vjp(norm_rows, after_attn, cross_gain, cross_shift)[1]
    grad_into_two, grad_cross_gain, grad_cross_shift = cross_norm_pull(grad_normed_two)
    grad_attn_res = grad_cross_res + grad_into_two
    grad_attn_low = grad_attn_res.astype(BF16)
    grad_heads = dot_nt(grad_attn_low, attn_weight).astype(BF16).reshape(seq_count, tok_rows, D)
    do_pair, do_single = heads_out(grad_heads, seq_count, tok_rows)
    do_pair, do_single = swap_all(do_pair), swap_all(do_single)
    grad_attn = dot_tn(attn_low, grad_attn_low)
    others = add_up(
        by_columns(
            jnp.concatenate(
                [grad_attn, grad_query, grad_cross, grad_memory, jnp.zeros((D, PAIR * 2), F32)], axis=1
            ),
            batch,
            seq_count,
        )
    )
    d_pair = pair_backward(first, do_pair, o_pair_t, lse_pair, cos_t, sin_t, cosine, sine)
    d_pair = swap_all(d_pair)
    d_single = single_backward(second, do_single, o_single_t, lse_single, cos_t, sin_t, cosine, sine)
    d_single = swap_all(d_single)
    pair_parts = d_pair.reshape(peers, 3, tok_rows, PAIR)
    both = d_single[:, :tok_rows].reshape(GROUPS, seq_count, tok_rows, 2, HD)
    both = both.transpose(3, 1, 2, 0, 4).reshape(2, seq_count, tok_rows, GROUPS * HD)

    def pair_rows(k):
        return (
            pair_parts[:, k]
            .reshape(GROUPS, seq_count, tok_rows, PAIR)
            .transpose(1, 2, 0, 3)
            .reshape(seq_count, tok_rows, GROUPS * PAIR)
        )

    grad_proj = jnp.concatenate(
        [
            heads_in(pair_parts[:, 0], d_single[:, tok_rows:], seq_count, tok_rows),
            pair_rows(1),
            both[0],
            pair_rows(2),
            both[1],
        ],
        axis=-1,
    ).reshape(all_rows, 3 * D)
    grad_qkv = dot_tn(normed_one, grad_proj)
    attn_norm_pull = jax.vjp(norm_rows, token_vals, attn_gain, attn_shift)[1]
    grad_into_one, grad_attn_gain, grad_attn_shift = attn_norm_pull(dot_nt(grad_proj, qkv_weight))
    grad_tokens = (grad_attn_res + grad_into_one).astype(BF16).reshape(seq_count, tok_rows, D)
    vectors = jnp.stack(
        [
            grad_attn_gain,
            grad_attn_shift,
            grad_cross_gain,
            grad_cross_shift,
            grad_mlp_gain,
            grad_mlp_shift,
        ],
        axis=1,
    )
    last = add_up(
        by_columns(
            jnp.concatenate(
                [grad_qkv, jnp.pad(vectors, ((0, 0), (0, 2 * PAIR - vectors.shape[1])))], axis=1
            ),
            batch,
            seq_count,
        )
    )
    own = D // peers

    def columns(value):
        return value.transpose(1, 0, 2).reshape(own, -1).astype(F32)

    deep = FF // peers // batch
    feed = feed.reshape(batch, 2, deep * D)
    grad_up = columns(feed[:, 0].reshape(batch, own, FF // batch))
    grad_down = feed[:, 1].reshape(batch * deep, D).astype(F32)
    others = columns(others)
    last = columns(last)
    return (
        output,
        grad_tokens,
        grad_neighbours,
        last[:, : 3 * D],
        others[:, :D],
        others[:, D : 2 * D],
        others[:, 3 * D : 5 * D],
        others[:, 2 * D : 3 * D],
        grad_up,
        grad_down,
    ) + tuple(last[:, 3 * D + k] for k in range(6))


def solution(mesh):
    batch, seq = mesh.shape["batch"], mesh.shape["seq"]
    fine = Mesh(
        mesh.devices.reshape(batch // 2, 2, GROUPS, seq // GROUPS), ("by", "bx", "hg", "sq")
    )
    rows = P(BATCH, SEQ, None)
    windows = P(BATCH, SEQ, None, None, None)
    return jax.shard_map(
        shards,
        mesh=fine,
        in_specs=(rows, windows, rows) + (P(),) * 13 + (rows,),
        out_specs=(rows, rows, windows) + (P(SEQ, None),) * 7 + (P(SEQ),) * 6,
        check_vma=False,
    )
```

time: 1060 us -> 702 us (0.66)
  waiting for transfers between devices: 526 us -> 84.3 us
  Pallas kernels: 0 us -> 105 us
  matrix products: 178 us -> 116 us
  starting transfers between devices: 15.8 us -> 60.2 us
  other arithmetic: 74.4 us -> 49.6 us
  blocking collectives: 37.4 us -> 51.4 us
  local copies, waits for them, and re-layouts: 198 us -> 209 us
    reduce_scatter x7 -> x3, waiting for transfers between devices: 386 us -> 13.9 us  [add_up(): lax.psum_scatter(flat, BATCH + ('sq',), scatter_dimension=0, tiled=True)]
    pallas_call x0 -> x5, Pallas kernels: none -> 105 us  [the longest x1 30.6 us: pair_backward(): pl.pallas_call(lambda *refs: pair_backward_body(rows, peers, *refs), grid...]
    all_gather x2 -> x1, waiting for transfers between devices: 90 us -> 0.01 us  [add_up(): return lax.all_gather(total, BATCH, axis=0)]
    all_to_all x0 -> x10, waiting for transfers between devices: none -> 67 us  [the longest x7 38.1 us: swap_all(): return lax.all_to_all(value, SEQ, 0, 0, tiled=True)]
    dot_general x28 -> x20, matrix products: 157 us -> 92.6 us  [the longest x7 37.1 us: dot_nt(): lax.dot_general(left, right, (((1,), (1,)), ((), ())), preferred_element_...]
    all_to_all x0 -> x10, starting transfers between devices: none -> 44.5 us  [the longest x7 31.5 us: swap_all(): return lax.all_to_all(value, SEQ, 0, 0, tiled=True)]
    dynamic_update_slice x8 -> x0, local copies, waits for them, and re-layouts: 33.8 us -> none  [shards(): lax.map(key_visit_block, jnp.arange(lax.axis_size('seq') * tok_rows // bl...]
    all_to_all x0 -> x1, blocking collectives: none -> 27.4 us  [swap_all(): return lax.all_to_all(value, SEQ, 0, 0, tiled=True)]
  transfers between devices with their start and end apart: 15 -> 18, of which waited for: 14 -> 8; matrix products, arithmetic and copies ran while one was open for 20% -> 39% of each run, Pallas kernels for 0% -> 14%
where the time goes in v1:
time: 702 us; the launch traced here: 690 us
  local copies, waits for them, and re-layouts  209 us (30%)
  matrix products  116 us (17%)
  Pallas kernels  105 us (15%)
  waiting for transfers between devices  84.3 us (12%)
  starting transfers between devices  60.2 us (9%)
  blocking collectives  51.4 us (7%)
  other arithmetic  49.6 us (7%)
  between operations  15.4 us (2%)
    all_to_all x7, waiting for transfers between devices, swap_all(): return lax.all_to_all(value, SEQ, 0, 0, tiled=True)  38.1 us
    dot_general x7, matrix products, dot_nt(): lax.dot_general(left, right, (((1,), (1,)), ((), ())), preferred_element_...  37.1 us
    all_to_all x7, starting transfers between devices, swap_all(): return lax.all_to_all(value, SEQ, 0, 0, tiled=True)  31.5 us
    pallas_call x1, Pallas kernels, pair_backward(): pl.pallas_call(lambda *refs: pair_backward_body(rows, peers, *refs), grid...  30.6 us
    all_to_all x3, waiting for transfers between devices, add_up(): parts = lax.all_to_all(own, 'hg', 0, 0, tiled=True)  29 us
    dot_general x6, matrix products, dot(): return jnp.dot(left, right, preferred_element_type=F32)  28.2 us
    pallas_call x1, Pallas kernels, pair_forward(): pl.pallas_call(lambda *refs: pair_forward_body(rows, peers, *refs), grid=...  27.5 us
    all_to_all x1, blocking collectives, swap_all(): return lax.all_to_all(value, SEQ, 0, 0, tiled=True)  27.4 us
  transfers between devices with their start and end apart: 18, of which 8 were waited for; matrix products, arithmetic and copies ran while one was open for 39% of the time, Pallas kernels for 14%

profile of v1, /device:TPU:0, one launch (start us, length us, event | category | flops | bytes accessed | tf_op | source)
XLA Modules:
  0.0 690.4 jit_solution(17368499322269875928)
XLA Ops:
  16.4 27.4 %all_to_all.55.refs_0_ = bf16[8,384,128]{2,1,0:T(8,128)(2,1)} all-to-all(bf16[8,384,128]{2,1,0:T(8,128)(2,1)} %bitcast.307), channel_id=1, replica_groups=mesh['by'=2,'bx'=2,'hg'=4,'sq'=2] {'hg','sq'}, dimensions={0} | all-to-all | bytes 1572864 | tf_op jit(solution)/shard_map/all_to_all | solution.py:560
  48.1 18.6 %attend_single.1 = (bf16[8,128,128]{2,1,0:T(8,128)(2,1)}, f32[64,2048]{1,0:T(8,128)}, f32[8,8,256]{2,1,0:T(8,128)}) custom-call(bf16[8,384,128]{2,1,0:T(8,128)(2,1)} %all_to_all.55.refs_0_), custom_call_target="tpu_custom_call" | custom-call | tf_op jit(solution)/shard_map/attend_single/pallas_call | solution.py:300
  66.7 19.2 %all-to-all-done.refs_0_ = bf16[8,768,128]{2,1,0:T(8,128)(2,1)} async-done(((bf16[8,768,128]{2,1,0:T(8,128)(2,1)}), bf16[8,768,128]{2,1,0:T(8,128)(2,1)}, u32[]{:S(2)}, u32[]{:S(2)}) %all-to-all-start) | async-done | bytes 1572896 | tf_op jit(solution)/shard_map/all_to_all | solution.py:560
  89.3 27.5 %attend_pair.1 = (bf16[2048,128]{1,0:T(8,128)(2,1)}, f32[128,2048]{1,0:T(8,128)}, f32[8,8,256]{2,1,0:T(8,128)}) custom-call(bf16[8,768,128]{2,1,0:T(8,128)(2,1)} %all-to-all-done.refs_0_), custom_call_target="tpu_custom_call" | custom-call | tf_op jit(solution)/shard_map/attend_pair/pallas_call | solution.py:250
  122.0 8.6 %convolution_convert_fusion = bf16[2048,1536]{1,0:T(8,128)(2,1)} fusion(bf16[2048,768]{1,0:T(8,128)(2,1)S(1)} %bitcast.262, bf16[768,1536]{1,0:T(8,128)(2,1)} %param.27), kind=kOutput, calls=%fused_computation.6 | convolution fusion | flops 4834983936 | bytes 11796480 | tf_op jit(solution)/shard_map/dot_general | solution.py:38
  130.5 8.7 %copy.145 = bf16[2048,1536]{0,1:T(8,128)(2,1)} copy(bf16[2048,1536]{1,0:T(8,128)(2,1)} %convolution_convert_fusion) | data formatting | bytes 12582912 | tf_op jit(solution)/shard_map/convert_element_type | solution.py:659
  139.2 11.2 %reshape.363 = bf16[2,4,256,2,12,64]{2,1,0,5,4,3:T(4,128)(2,1)} reshape(bf16[2048,1536]{0,1:T(8,128)(2,1)} %copy.145) | data formatting | bytes 12582912 | tf_op jit(solution)/shard_map/reshape | solution.py:660
  214.4 17.1 %add_convert_fusion = (bf16[512,3072]{1,0:T(8,128)(2,1)S(1)}, f32[512,3072]{1,0:T(8,128)S(1)}) fusion(f32[512,3072]{1,0:T(8,128)S(1)} %fusion.63, bf16[512,768]{1,0:T(8,128)(2,1)S(1)} %bitcast.282, bf16[3072,768]{1,0:T(8,128)(2,1)S(1)} %bitcast.320), kind=kOutput, calls=%fused_computation.19 | convolution fusion | flops 2529165312 | bytes 21233664 | tf_op jit(solution)/shard_map/dot_general | solution.py:42
  248.7 9.2 %collective-permute-start.2 = (bf16[2,1,768]{1,2,0:T(8,128)(2,1)S(1)}, bf16[2,1,768]{1,2,0:T(8,128)(2,1)}, u32[]{:S(2)}, u32[]{:S(2)}) collective-permute-start(bf16[2,1,768]{1,2,0:T(8,128)(2,1)S(1)} %copy.201), channel_id=1, source_target_pairs={{0,1},{1,2},{2,3},{3,4},{4,5},{5,6},{6,7},{8,9},{9,10},{10,11},{11... | collective-permute-start | bytes 9224 | tf_op jit(solution)/shard_map/ppermute | solution.py:541
  265.2 9.9 %reshape.388 = bf16[4,2,96,4,768]{4,3,2,1,0:T(4,128)(2,1)} reshape(bf16[768,3072]{1,0:T(8,128)(2,1)} %convolution_convert_fusion.2) | data formatting | bytes 9437184 | tf_op jit(solution)/shard_map/reshape | solution.py:599
  291.1 9.4 %fusion.3 = (f32[2,4,64,12]{2,3,1,0:T(8,128)S(1)}, f32[2,4,12,256,64]{3,4,2,1,0:T(8,128)S(1)}) fusion(f32[2,4,64,12,256]{4,2,3,1,0:T(8,128)} %copy-done.14, f32[2,4,64,12]{2,3,1,0:T(8,128)S(1)} %copy-done.39, bf16[2,4,256,1,12,64]{2,1,0,5,4,3:T(4,128)(2,1)} %get-tuple-element.56, bf16[2,4,64,12,64]{2,1,4,3,0:T(4,128)(2,1)} %reshape.372), kind=kOutput, calls=%fused_computation.10 | convolution fusion | flops 206039040 | bytes 16564224 | tf_op jit(solution)/shard_map/scqhd,sckhd->scqhk/dot_general | solution.py:711
  348.5 21.5 %attend_single_grads.1 = bf16[8,384,128]{2,1,0:T(8,128)(2,1)} custom-call(bf16[8,384,128]{2,1,0:T(8,128)(2,1)} %all_to_all.55.refs_0_, bf16[8,128,128]{2,1,0:T(8,128)(2,1)} %copy-done.28, f32[64,2048]{1,0:T(8,128)} %get-tuple-element.30.refs_2_, f32[8,8,256]{2,1,0:T(8,128)} %get-tuple-element.31.refs_3_, f32[32,2048]{1,0:T(8,128)} %constant.121.clone.refs_4_, ...), custom_call_target="tpu_custom_call" | custom-call | tf_op jit(solution)/shard_map/attend_single_grads/pallas_call | solution.py:511
  375.0 30.6 %attend_pair_grads.1 = bf16[8,768,128]{2,1,0:T(8,128)(2,1)} custom-call(bf16[8,768,128]{2,1,0:T(8,128)(2,1)} %all-to-all-done.refs_0_, bf16[8,256,128]{2,1,0:T(8,128)(2,1)} %all-to-all-done.4.refs_1_, f32[128,2048]{1,0:T(8,128)} %get-tuple-element.28.refs_2_, f32[8,8,256]{2,1,0:T(8,128)} %get-tuple-element.29.refs_3_, f32[32,2048]{1,0:T(8,128)} %constant.121.clone.refs_4_, ...), custom_call_target="tpu_custom_call" | custom-call | tf_op jit(solution)/shard_map/attend_pair_grads/pallas_call | solution.py:414
  433.5 15.1 %all-to-all-done.5 = bf16[8,768,128]{2,1,0:T(8,128)(2,1)} async-done(((bf16[8,768,128]{2,1,0:T(8,128)(2,1)}), bf16[8,768,128]{2,1,0:T(8,128)(2,1)}, u32[]{:S(2)}, u32[]{:S(2)}) %all-to-all-start.5) | async-done | bytes 1572896 | tf_op jit(solution)/shard_map/all_to_all | solution.py:560
  491.3 11.1 %copy.178 = bf16[2,4,256,2,12,64]{2,1,0,5,4,3:T(4,128)(2,1)} copy(bf16[2,4,256,2,12,64]{2,5,4,1,0,3:T(8,128)(2,1)} %maximum_convert_fusion) | data formatting | bytes 12582912 | tf_op jit(solution)/shard_map/convert_element_type | solution.py:734
  502.4 11.1 %convert_element_type.161 = bf16[2048,1536]{0,1:T(8,128)(2,1)} reshape(bf16[2,4,256,2,12,64]{2,1,0,5,4,3:T(4,128)(2,1)} %copy.178) | data formatting | bytes 12582912 | tf_op jit(solution)/shard_map/convert_element_type | solution.py:734
  531.9 8.6 %copy.183 = bf16[768,4096]{1,0:T(8,128)(2,1)} copy(bf16[768,4096]{0,1:T(8,128)(2,1)} %broadcast_dynamic-update-slice_fusion) | data formatting | bytes 12582912 | tf_op jit(solution)/shard_map/concatenate | solution.py:755
  540.5 11.2 %convert_element_type.168 = bf16[4,2,96,4,1024]{4,3,2,1,0:T(4,128)(2,1)} reshape(bf16[768,4096]{1,0:T(8,128)(2,1)} %copy.183) | data formatting | bytes 12582912 | tf_op jit(solution)/shard_map/convert_element_type | solution.py:599
  563.6 28.9 %all-to-all-done.10 = bf16[4,192,768]{2,1,0:T(8,128)(2,1)} async-done(((bf16[4,192,768]{2,1,0:T(8,128)(2,1)}), bf16[4,192,768]{2,1,0:T(8,128)(2,1)}, u32[]{:S(2)}, u32[]{:S(2)}) %all-to-all-start.10) | async-done | bytes 1179680 | tf_op jit(solution)/shard_map/all_to_all | solution.py:592
  606.3 13.8 %reduce-scatter.6.cloned.1.call-done = bf16[1,4,96,1024]{3,2,1,0:T(8,128)(2,1)} async-done(((bf16[8,4,96,1024]{3,2,1,0:T(8,128)(2,1)}), bf16[1,4,96,1024]{3,2,1,0:T(8,128)(2,1)}) %reduce-scatter.6.cloned.1.call-update) | async-done | bytes 786448 | tf_op jit(solution)/shard_map/reduce_scatter | solution.py:590
  624.8 9.2 %convolution_convert_fusion.5 = bf16[2048,768]{1,0:T(8,128)(2,1)} fusion(bf16[2048,1536]{0,1:T(8,128)(2,1)} %convert_element_type.161, bf16[768,1536]{1,0:T(8,128)(2,1)} %param.27), kind=kOutput, calls=%fused_computation.42 | convolution fusion | flops 4833411072 | bytes 11796480 | tf_op jit(solution)/shard_map/dot_general | solution.py:42
  636.6 12.6 %all-gather = bf16[384,640]{1,0:T(8,128)(2,1)S(1)} all-gather(bf16[96,640]{1,0:T(8,128)(2,1)S(1)} %reduce_sum.286), channel_id=2, replica_groups=mesh['by'=2,'bx'=2,'hg'=4,'sq'=2] {'by','bx'}, dimensions={0}, use_global_device_ids=true | all-gather | bytes 614400 | tf_op jit(solution)/shard_map/all_gather | solution.py:594
  652.4 11.4 %all-gather.1 = bf16[384,1024]{1,0:T(8,128)(2,1)S(1)} all-gather(bf16[96,1024]{1,0:T(8,128)(2,1)S(1)} %reduce_sum.328), channel_id=3, replica_groups=mesh['by'=2,'bx'=2,'hg'=4,'sq'=2] {'by','bx'}, dimensions={0}, use_global_device_ids=true | all-gather | bytes 983040 | tf_op jit(solution)/shard_map/all_gather | solution.py:594
  669.5 9.5 %fusion.50 = (f32[4,73728]{1,0:T(4,128)}, f32[4,73728]{1,0:T(4,128)S(1)}) fusion(bf16[4,2,73728]{2,1,0:T(2,128)(2,1)} %reshape.392), kind=kLoop, calls=%fused_computation.110 | loop fusion | flops 589824 | bytes 3538944 | tf_op jit(solution)/shard_map/convert_element_type | solution.py:820
  (310 shorter events, 313.4 us)
Async XLA Ops:
  7.2 114.8 %copy-start = (bf16[2,4,2,128,768]{4,3,2,1,0:T(8,128)(2,1)S(1)}, bf16[2,4,2,128,768]{4,3,2,1,0:T(8,128)(2,1)}, u32[]{:S(2)}) copy-start(bf16[2,4,2,128,768]{4,3,2,1,0:T(8,128)(2,1)} %param.22) | copy-start | bytes 9437188
  43.8 42.1 %all-to-all-start = ((bf16[8,768,128]{2,1,0:T(8,128)(2,1)}), bf16[8,768,128]{2,1,0:T(8,128)(2,1)}, u32[]{:S(2)}, u32[]{:S(2)}) async-start(bf16[8,768,128]{2,1,0:T(8,128)(2,1)} %bitcast.295), calls=%async_computation | async-start | bytes 3145728 | tf_op jit(solution)/shard_map/all_to_all | solution.py:560
  85.9 31.0 %all-to-all-start.3 = ((bf16[8,128,128]{2,1,0:T(8,128)(2,1)}), bf16[8,128,128]{2,1,0:T(8,128)(2,1)S(1)}, u32[]{:S(2)}, u32[]{:S(2)}) async-start(bf16[8,128,128]{2,1,0:T(8,128)(2,1)} %get-tuple-element.27), calls=%async_computation.3 | async-start | bytes 524288 | tf_op jit(solution)/shard_map/all_to_all | solution.py:560
  116.9 13.6 %copy-start.29 = (bf16[8,128,128]{2,1,0:T(8,128)(2,1)}, bf16[8,128,128]{2,1,0:T(8,128)(2,1)S(1)}, u32[]{:S(2)}) copy-start(bf16[8,128,128]{2,1,0:T(8,128)(2,1)S(1)} %all-to-all-done.3) | copy-start | bytes 786436
  116.9 44.5 %all-to-all-start.1 = ((bf16[8,256,128]{2,1,0:T(8,128)(2,1)}), bf16[8,256,128]{2,1,0:T(8,128)(2,1)}, u32[]{:S(2)}, u32[]{:S(2)}) async-start(bf16[8,256,128]{2,1,0:T(8,128)(2,1)} %bitcast.311), calls=%async_computation.1 | async-start | bytes 1048576 | tf_op jit(solution)/shard_map/all_to_all | solution.py:560
  121.9 437.3 %reduce-scatter.8.cloned.1.call-start = ((), (), s32[]{:S(2)}) async-start(), calls=%async_computation.16 | async-start | bytes 10616832 | tf_op jit(solution)/shard_map/reduce_scatter | solution.py:590
  139.2 11.2 %copy-start.53 = (s32[2,4,2]{1,2,0:T(2,128)S(1)}, s32[2,4,2]{1,2,0:T(2,128)}, u32[]{:S(2)}) copy-start(s32[2,4,2]{1,2,0:T(2,128)} %param.23) | copy-start | bytes 196
  167.3 3.2 collective-permute-start
  197.8 4.7 collective-permute-start.1
  209.0 35.2 %copy-start.6 = (f32[512,768]{1,0:T(8,128)}, f32[512,768]{1,0:T(8,128)S(1)}, u32[]{:S(2)}) copy-start(f32[512,768]{1,0:T(8,128)S(1)} %get-tuple-element.77) | copy-start | bytes 4718596
  209.4 22.2 %slice-start = ((s8[4718592]{0:T(1024)(128)(4,1)}), s8[4194304]{0:T(1024)(128)(4,1)S(1)}, s32[]{:S(2)}) async-start(s8[4718592]{0:T(1024)(128)(4,1)} %bitcast.317), calls=%async_computation.18 | async-start | bytes 8388608
  214.4 17.2 %slice-start.1 = ((s8[4718592]{0:T(1024)(128)(4,1)}), s8[524288]{0:T(1024)(128)(4,1)S(1)}, s32[]{:S(2)}) async-start(s8[4718592]{0:T(1024)(128)(4,1)} %bitcast.317), calls=%async_computation.19 | async-start | bytes 1048576
  248.7 36.3 %collective-permute-start.2 = (bf16[2,1,768]{1,2,0:T(8,128)(2,1)S(1)}, bf16[2,1,768]{1,2,0:T(8,128)(2,1)}, u32[]{:S(2)}, u32[]{:S(2)}) collective-permute-start(bf16[2,1,768]{1,2,0:T(8,128)(2,1)S(1)} %copy.201), channel_id=1, source_target_pairs={{0,1},{1,2},{2,3},{3,4},{4,5},{5,6},{6,7},{8,9},{9,10},{10,11},{11... | collective-permute-start | bytes 9224 | tf_op jit(solution)/shard_map/ppermute | solution.py:541
  316.7 3.2 collective-permute-start.3
  330.1 14.3 %all-to-all-start.6 = ((bf16[8,128,128]{2,1,0:T(8,128)(2,1)}), bf16[8,128,128]{2,1,0:T(8,128)(2,1)S(1)}, u32[]{:S(2)}, u32[]{:S(2)}) async-start(bf16[8,128,128]{2,1,0:T(8,128)(2,1)} %copy.163), calls=%async_computation.6 | async-start | bytes 524288 | tf_op jit(solution)/shard_map/all_to_all | solution.py:560
  344.3 25.6 %all-to-all-start.4 = ((bf16[8,256,128]{2,1,0:T(8,128)(2,1)}), bf16[8,256,128]{2,1,0:T(8,128)(2,1)}, u32[]{:S(2)}, u32[]{:S(2)}) async-start(bf16[8,256,128]{2,1,0:T(8,128)(2,1)} %bitcast.284), calls=%async_computation.4 | async-start | bytes 1048576 | tf_op jit(solution)/shard_map/all_to_all | solution.py:560
  370.0 35.6 %all-to-all-start.7 = ((bf16[8,384,128]{2,1,0:T(8,128)(2,1)}), bf16[8,384,128]{2,1,0:T(8,128)(2,1)}, u32[]{:S(2)}, u32[]{:S(2)}) async-start(bf16[8,384,128]{2,1,0:T(8,128)(2,1)} %attend_single_grads.1), calls=%async_computation.7 | async-start | bytes 1572864 | tf_op jit(solution)/shard_map/all_to_all | solution.py:560
  405.5 43.0 %all-to-all-start.5 = ((bf16[8,768,128]{2,1,0:T(8,128)(2,1)}), bf16[8,768,128]{2,1,0:T(8,128)(2,1)}, u32[]{:S(2)}, u32[]{:S(2)}) async-start(bf16[8,768,128]{2,1,0:T(8,128)(2,1)} %attend_pair_grads.1), calls=%async_computation.5 | async-start | bytes 3145728 | tf_op jit(solution)/shard_map/all_to_all | solution.py:560
  410.7 152.9 %reduce-scatter.4.cloned.1.call-start = ((), (), s32[]{:S(2)}) async-start(), calls=%async_computation.14 | async-start | bytes 4423680 | tf_op jit(solution)/shard_map/reduce_scatter | solution.py:590
  476.7 143.4 %reduce-scatter.6.cloned.1.call-start = ((), (), s32[]{:S(2)}) async-start(), calls=%async_computation.15 | async-start | bytes 7077888 | tf_op jit(solution)/shard_map/reduce_scatter | solution.py:590
  559.3 33.3 %all-to-all-start.10 = ((bf16[4,192,768]{2,1,0:T(8,128)(2,1)}), bf16[4,192,768]{2,1,0:T(8,128)(2,1)}, u32[]{:S(2)}, u32[]{:S(2)}) async-start(bf16[4,192,768]{2,1,0:T(8,128)(2,1)} %bitcast.296), calls=%async_computation.13 | async-start | bytes 2359296 | tf_op jit(solution)/shard_map/all_to_all | solution.py:592
  592.5 27.6 %all-to-all-start.8 = ((bf16[4,96,640]{2,1,0:T(8,128)(2,1)}), bf16[4,96,640]{2,1,0:T(8,128)(2,1)}, u32[]{:S(2)}, u32[]{:S(2)}) async-start(bf16[4,96,640]{2,1,0:T(8,128)(2,1)} %bitcast.312), calls=%async_computation.9 | async-start | bytes 983040 | tf_op jit(solution)/shard_map/all_to_all | solution.py:592
  596.7 69.3 %all-gather.5.cloned.1.call-start = ((), (), s32[]{:S(2)}) async-start(), calls=%async_computation.17 | async-start | bytes 1474560 | tf_op jit(solution)/shard_map/all_gather | solution.py:594
  620.2 31.0 %all-to-all-start.9 = ((bf16[4,96,1024]{2,1,0:T(8,128)(2,1)}), bf16[4,96,1024]{2,1,0:T(8,128)(2,1)}, u32[]{:S(2)}, u32[]{:S(2)}) async-start(bf16[4,96,1024]{2,1,0:T(8,128)(2,1)} %bitcast.306), calls=%async_computation.11 | async-start | bytes 1572864 | tf_op jit(solution)/shard_map/all_to_all | solution.py:592
  (56 other events, 194.0 us)
Sparse Core Ops, SparseCore 0:
  285.1 75.7 reduce-scatter.7
  476.9 49.0 reduce-scatter.3
  559.4 60.7 reduce-scatter.5
  622.4 29.6 all-gather.4
